TPU v7x, 768 devices: a whole 4x8x12 slice. The times are simulated.
768 devices in a mesh: context: 24 (over z, core), channel: 8 (over y), dp: 4 (over x).
Axes of the slice: x: 4, y: 8, z: 12, core: 2. Of those that a mesh axis runs over, the one named last changes fastest.
Arguments:
- features: bfloat16 [4, 12288, 3, 2048], P('dp', 'context', None, 'channel'), may hold values from -6 to 6
- doc_start: int32 [4, 24], P('dp'), may hold values 0 or 1
- short_taps: float32 [3, 3, 2048], P(None, None, 'channel'), may hold values from -3 to 3
- long_filter: bfloat16 [2048, 2048], P('channel', 'dp'), may hold values from -0.125 to 0.125
- w_out: bfloat16 [2048, 2048], P('channel'), may hold values from -0.125 to 0.125
Outputs:
- layer_out: bfloat16 [4, 12288, 2048], P('dp', ('context', 'channel'))
Inputs may be any that keep to these rules, and one draw needn't show every extreme that they name: `doc_start`: block 0 of every sequence begins a document whatever its entry.
All inputs are finite; a program needn't handle non-finite values.
Results may differ from a plain program's by a relative error of at most 0.023.
Values may be sent and summed in bfloat16 or wider, within the bound.
A program may use at most 64 MiB of HBM per device.

v0:
```python
import functools

import jax
import jax.numpy as jnp
import numpy as np
from jax import lax
from jax.experimental import pallas as pl
from jax.experimental.pallas import tpu as pltpu
from jax.sharding import PartitionSpec as P

MESH = pl.DeviceIdType.MESH
F32 = jnp.float32
BF16 = jnp.bfloat16
HALF = 128


def tables(block_len):
    freq = np.concatenate([np.arange(0, block_len, 2), np.arange(1, block_len, 2)])
    angle = 2.0 * np.pi * ((2 * freq[:, None] + 1) * np.arange(block_len)[None, :] % (4 * block_len)) / (4 * block_len)
    sign = np.where(freq % 2 == 0, 1.0, -1.0)[:, None]
    forward = np.concatenate([np.cos(angle), -np.sin(angle)], 0)
    inverse = np.concatenate([-sign * np.sin(angle), -sign * np.cos(angle)], 0).T / block_len
    return forward.astype(jnp.bfloat16), inverse.astype(jnp.bfloat16)


def kernel(
    sizes, doc, taps, x, filt, w, fwd, inv, out,
    ext, fbuf, ibuf, wbuf, pbuf, rbuf, tbuf, fspec, gspec, spec, qbuf, acc, total, cown, csend, crecv, gated, sbuf, vbuf,
    load_sem, tail_sem, tap_send, tap_recv, halo_send, halo_recv, swap_send, swap_recv, ring_send, ring_recv,
):
    n_ctx, n_ch, n_dp, block_len, d_out = sizes
    chips = n_ctx // 2
    ctx = lax.axis_index("context")
    y = lax.axis_index("channel")
    xi = lax.axis_index("dp")
    z = ctx // 2
    c = ctx % 2
    piece = block_len // n_ch
    sub = d_out // 4
    steps = n_ch - 1

    def chip(distance):
        return lax.rem(z + distance + chips, chips)

    barrier = pltpu.get_barrier_semaphore()
    pl.semaphore_signal(barrier, inc=1, device_id={"context": 2 * z + 1 - c}, device_id_type=MESH)
    for distance in (-1, -2):
        for core in (0, 1):
            pl.semaphore_signal(barrier, inc=1, device_id={"context": 2 * chip(distance) + core}, device_id_type=MESH)
    for by in range(1, n_dp):
        pl.semaphore_signal(barrier, inc=1, device_id={"dp": lax.rem(xi + by, n_dp)}, device_id_type=MESH)
    for by in (1, n_ch - 1):
        pl.semaphore_signal(barrier, inc=1, device_id={"channel": lax.rem(y + by, n_ch)}, device_id_type=MESH)

    own_rows = pl.ds(pl.multiple_of(c * HALF, HALF), HALF)
    loads = [
        pltpu.make_async_copy(x, ext.at[:, pl.ds(16, block_len), :], load_sem.at[0]),
        pltpu.make_async_copy(filt.at[own_rows, :], tbuf.at[xi], load_sem.at[1]),
        pltpu.make_async_copy(fwd, fbuf, load_sem.at[2]),
        pltpu.make_async_copy(inv, ibuf, load_sem.at[3]),
        pltpu.make_async_copy(w, wbuf, load_sem.at[4]),
    ]
    for load in loads:
        load.start()
    pl.semaphore_wait(barrier, 4 + n_dp + 2)

    tail = pltpu.make_async_remote_copy(
        src_ref=x.at[:, pl.ds(block_len - 16, 16), :], dst_ref=ext.at[:, pl.ds(0, 16), :],
        send_sem=tail_sem.at[0], recv_sem=tail_sem.at[1],
        device_id={"context": lax.rem(ctx + 1, n_ctx)}, device_id_type=MESH)
    tail.start()

    def tap_copy(by):
        return pltpu.make_async_remote_copy(
            src_ref=filt.at[own_rows, :], dst_ref=tbuf.at[xi],
            send_sem=tap_send.at[by - 1], recv_sem=tap_recv.at[by - 1],
            device_id={"dp": lax.rem(xi + by, n_dp)}, device_id_type=MESH)

    for by in range(1, n_dp):
        tap_copy(by).start()

    def goes_on(block):
        at = jnp.maximum(block, 0)
        return jnp.where((block > 0) & (doc[0, at] != 1), 1.0, 0.0).astype(F32)

    own_goes_on = goes_on(ctx)
    keep_b = goes_on(2 * z + 1)
    keep1 = goes_on(2 * z)
    keep2 = keep1 * goes_on(2 * z - 1)
    keep3 = keep2 * goes_on(2 * z - 2)
    keep4 = keep3 * goes_on(2 * z - 3)

    chunk = min(128, block_len)

    def smooth(stream, start):
        rows = ext[stream, pl.ds(start, chunk + 16), :].astype(F32)
        got = (
            taps[0, pl.ds(stream, 1), :] * rows
            + taps[1, pl.ds(stream, 1), :] * pltpu.roll(rows, 1, 0)
            + taps[2, pl.ds(stream, 1), :] * pltpu.roll(rows, 2, 0)
        )
        return got[16:]

    def make_product(start):
        product = (smooth(1, start) * smooth(2, start)).astype(BF16)
        pbuf[0, pl.ds(start, chunk), :] = product[:, :HALF]
        pbuf[1, pl.ds(start, chunk), :] = product[:, HALF:]

    loads[0].wait()
    for start in range(chunk, block_len, chunk):
        make_product(start)
    tail.wait_recv()
    for stream in range(3):
        ext[stream, pl.ds(0, 16), :] = (ext[stream, pl.ds(0, 16), :].astype(F32) * own_goes_on).astype(BF16)
    make_product(0)

    def halo_copy(distance, half):
        return pltpu.make_async_remote_copy(
            src_ref=pbuf.at[half], dst_ref=rbuf.at[distance, c],
            send_sem=halo_send.at[distance, half], recv_sem=halo_recv.at[distance, c],
            device_id={"context": 2 * chip(distance) + half}, device_id_type=MESH)

    def halo_arrived(distance, core):
        pltpu.make_async_remote_copy(
            src_ref=pbuf.at[0], dst_ref=rbuf.at[distance, core],
            send_sem=halo_send.at[distance, 0], recv_sem=halo_recv.at[distance, core],
            device_id={"context": ctx}, device_id_type=MESH).wait_recv()

    halo_copy(0, 1 - c).start()
    for distance in (1, 2):
        for half in (0, 1):
            halo_copy(distance, half).start()
    rbuf[0, c] = pbuf[c]

    for start in range(0, block_len, chunk):
        smoothed = smooth(0, start)
        qbuf[0, pl.ds(start, chunk), :] = smoothed[:, :HALF]
        qbuf[1, pl.ds(start, chunk), :] = smoothed[:, HALF:]

    loads[1].wait()
    loads[2].wait()
    for by in range(1, n_dp):
        tap_copy(by).wait_recv()
    taps_all = tbuf[...].reshape(n_dp * HALF, block_len)
    tile = block_len // 2

    def filter_rows(i, carry):
        rows = pl.ds(pl.multiple_of(i * tile, tile), tile)
        fspec[rows, :] = lax.dot_general(
            fbuf[rows, :], tbuf[...].reshape(n_dp * HALF, block_len), (((1,), (1,)), ((), ())), preferred_element_type=F32)
        return carry

    lax.fori_loop(0, 4, filter_rows, 0)

    step_rows = min(64, block_len // 2)
    tiles = block_len // step_rows

    def places(i):
        at = pl.multiple_of(i * step_rows, step_rows)
        return pl.ds(at, step_rows), pl.ds(block_len + at, step_rows)

    def combine(i, carry):
        re, im = places(i)
        sign = (1 - 2 * (i // (tiles // 2))).astype(F32)
        for d in range(n_dp + 1):
            real = imag = None
            if d > 0:
                lanes = pl.ds((d - 1) * HALF, HALF)
                real, imag = fspec[re, lanes], fspec[im, lanes]
            if d < n_dp:
                lanes = pl.ds(d * HALF, HALF)
                more_real, more_imag = sign * fspec[im, lanes], -sign * fspec[re, lanes]
                real = more_real if real is None else real + more_real
                imag = more_imag if imag is None else imag + more_imag
            gspec[d, re, :] = real
            gspec[d, im, :] = imag
        return carry

    lax.fori_loop(0, tiles, combine, 0)

    def transform(distance, keep_lo, keep_hi):
        lo, hi = rbuf[distance, 0], rbuf[distance, 1]
        if keep_lo is not None:
            lo = (lo.astype(F32) * keep_lo).astype(BF16)
            hi = (hi.astype(F32) * keep_hi).astype(BF16)
        rbuf[distance, 0] = lo
        rbuf[distance, 1] = hi

        def rows_of(i, carry):
            rows = pl.ds(pl.multiple_of(i * tile, tile), tile)
            both = jnp.concatenate([rbuf[distance, 0], rbuf[distance, 1]], 1)
            spec[distance, rows, :] = jnp.dot(fbuf[rows, :], both, preferred_element_type=F32)
            return carry

        lax.fori_loop(0, 4, rows_of, 0)

    def term(d, distance, core, re, im):
        lanes = pl.ds(core * HALF, HALF)
        a, b = gspec[d, re, :], gspec[d, im, :]
        u, v = spec[distance, re, lanes], spec[distance, im, lanes]
        return a * u - b * v, a * v + b * u

    def terms(which, re, im):
        got = [term(d, distance, core, re, im) for d, distance, core in which]
        return sum(g[0] for g in got[1:]) + got[0][0], sum(g[1] for g in got[1:]) + got[0][1]

    halo_arrived(0, 1 - c)
    transform(0, None, None)
    for core in (0, 1):
        halo_arrived(1, core)
    transform(1, keep2, keep1)

    def early(i, carry):
        re, im = places(i)
        real, imag = terms([(0, 0, 0), (1, 1, 1), (2, 1, 0)], re, im)
        acc[0, re, :] = real
        acc[0, im, :] = imag
        real, imag = terms([(1, 0, 0), (2, 1, 1), (3, 1, 0)], re, im)
        acc[1, re, :] = real
        acc[1, im, :] = imag
        return carry

    lax.fori_loop(0, tiles, early, 0)
    for core in (0, 1):
        halo_arrived(2, core)
    transform(2, keep4, keep3)

    def late(i, carry):
        re, im = places(i)
        real, imag = terms([(3, 2, 1), (4, 2, 0)], re, im)
        total[re, pl.ds(0, HALF)] = (acc[0, re, :] + real).astype(BF16)
        total[im, pl.ds(0, HALF)] = (acc[0, im, :] + imag).astype(BF16)
        real, imag = terms([(4, 2, 1)], re, im)
        own_real, own_imag = terms([(0, 0, 1)], re, im)
        total[re, pl.ds(HALF, HALF)] = (own_real + keep_b * (acc[1, re, :] + real)).astype(BF16)
        total[im, pl.ds(HALF, HALF)] = (own_imag + keep_b * (acc[1, im, :] + imag)).astype(BF16)
        return carry

    lax.fori_loop(0, tiles, late, 0)

    loads[3].wait()

    def swap_copy(i):
        rows = pl.ds(i * chunk, chunk)
        return pltpu.make_async_remote_copy(
            src_ref=csend.at[rows, :], dst_ref=crecv.at[rows, :],
            send_sem=swap_send.at[i], recv_sem=swap_recv.at[i],
            device_id={"context": 2 * z + 1 - c}, device_id_type=MESH)

    own_first = (1 - c).astype(F32)
    own_second = c.astype(F32)
    for i in range(block_len // chunk):
        rows = pl.ds(i * chunk, chunk)
        conv = jnp.dot(ibuf[rows, :], total[...], preferred_element_type=F32)
        cown[0, rows, :] = conv[:, :HALF]
        cown[1, rows, :] = conv[:, HALF:]
        csend[rows, :] = cown[1 - c, rows, :].astype(BF16)
        swap_copy(i).start()
        gated[c, rows, :] = (qbuf[c, rows, :] * cown[c, rows, :]).astype(BF16)
    for i in range(block_len // chunk):
        rows = pl.ds(i * chunk, chunk)
        swap_copy(i).wait_recv()
        gated[1 - c, rows, :] = (qbuf[1 - c, rows, :] * crecv[rows, :].astype(F32)).astype(BF16)

    loads[4].wait()

    def ring_copy(s, q):
        to = lax.rem(y + (1 if q < 2 else n_ch - 1), n_ch)
        return pltpu.make_async_remote_copy(
            src_ref=sbuf.at[s, q], dst_ref=vbuf.at[s, q],
            send_sem=ring_send.at[s, q], recv_sem=ring_recv.at[s, q],
            device_id={"channel": to}, device_id_type=MESH)

    def project(j, q):
        rows = pl.ds(pl.multiple_of(j * piece, piece), piece)
        lhs = jnp.concatenate([gated[0, rows, :], gated[1, rows, :]], 1)
        return jnp.dot(lhs, wbuf[:, q * sub:(q + 1) * sub], preferred_element_type=F32)

    def ring_step(s, first):
        up = lax.rem(y - 1 - s + 2 * n_ch, n_ch)
        down = lax.rem(y + 1 + s, n_ch)
        for q in (0, 2, 1, 3):
            part = project(up if q < 2 else down, q)
            if not first:
                ring_copy(s - 1, q).wait_recv()
                part = part + vbuf[s - 1, q].astype(F32)
            sbuf[s, q] = part.astype(BF16)
            ring_copy(s, q).start()

    ring_step(0, True)

    def ring_body(s, carry):
        ring_step(s, False)
        return carry

    lax.fori_loop(1, steps, ring_body, 0)
    for q in (0, 2, 1, 3):
        part = project(y, q)
        ring_copy(steps - 1, q).wait_recv()
        out[:, q * sub:(q + 1) * sub] = (part + vbuf[steps - 1, q].astype(F32)).astype(BF16)

    tail.wait_send()
    for by in range(1, n_dp):
        tap_copy(by).wait_send()
    halo_copy(0, 1 - c).wait_send()
    for distance in (1, 2):
        for half in (0, 1):
            halo_copy(distance, half).wait_send()
    for i in range(block_len // chunk):
        swap_copy(i).wait_send()

    def sent(s, carry):
        for q in range(4):
            ring_copy(s, q).wait_send()
        return carry

    lax.fori_loop(0, steps, sent, 0)


def per_device(mesh_shape, features, doc_start, short_taps, long_filter, w_out):
    block_len, channels, d_out = features.shape[1], features.shape[3], w_out.shape[1]
    n_ctx, n_ch, n_dp = mesh_shape["context"], mesh_shape["channel"], mesh_shape["dp"]
    streams = jnp.transpose(features[0], (1, 0, 2))
    forward, inverse = tables(block_len)
    piece, sub, steps = block_len // n_ch, d_out // 4, n_ch - 1
    width = 2 * block_len
    swaps = block_len // min(128, block_len)
    anywhere = pl.BlockSpec(memory_space=pl.ANY)
    vmem = pl.BlockSpec(memory_space=pltpu.VMEM)
    dma = pltpu.SemaphoreType.DMA
    result = pl.pallas_call(
        functools.partial(kernel, (n_ctx, n_ch, n_dp, block_len, d_out)),
        out_shape=jax.ShapeDtypeStruct((piece, d_out), BF16),
        in_specs=[pl.BlockSpec(memory_space=pltpu.SMEM), vmem] + [anywhere] * 5,
        out_specs=vmem,
        scratch_shapes=[
            pltpu.VMEM((3, 16 + block_len, channels), BF16),
            pltpu.VMEM((width, block_len), BF16),
            pltpu.VMEM((block_len, width), BF16),
            pltpu.VMEM((channels, d_out), BF16),
            pltpu.VMEM((2, block_len, HALF), BF16),
            pltpu.VMEM((3, 2, block_len, HALF), BF16),
            pltpu.VMEM((n_dp, HALF, block_len), BF16),
            pltpu.VMEM((width, n_dp * HALF), F32),
            pltpu.VMEM((n_dp + 1, width, HALF), F32),
            pltpu.VMEM((3, width, 2 * HALF), F32),
            pltpu.VMEM((2, block_len, HALF), F32),
            pltpu.VMEM((2, width, HALF), F32),
            pltpu.VMEM((width, 2 * HALF), BF16),
            pltpu.VMEM((2, block_len, HALF), F32),
            pltpu.VMEM((block_len, HALF), BF16),
            pltpu.VMEM((block_len, HALF), BF16),
            pltpu.VMEM((2, block_len, HALF), BF16),
            pltpu.VMEM((steps, 4, piece, sub), BF16),
            pltpu.VMEM((steps, 4, piece, sub), BF16),
            dma((5,)), dma((2,)), dma((n_dp - 1,)), dma((n_dp - 1,)), dma((3, 2)), dma((3, 2)),
            dma((swaps,)), dma((swaps,)), dma((steps, 4)), dma((steps, 4)),
        ],
        compiler_params=pltpu.CompilerParams(
            collective_id=0, has_side_effects=True, vmem_limit_bytes=48 * 1024 * 1024),
    )(doc_start, short_taps, streams, long_filter, w_out, forward, inverse)
    return result[None]


def solution(mesh):
    return jax.shard_map(
        functools.partial(per_device, dict(mesh.shape)),
        mesh=mesh,
        in_specs=(
            P("dp", "context", None, "channel"),
            P("dp", None),
            P(None, None, "channel"),
            P("channel", "dp"),
            P("channel", None),
        ),
        out_specs=P("dp", ("context", "channel"), None),
        check_vma=False,
    )
```

profile of v0, /device:TPU:8, one launch (start us, length us, event | category | flops | bytes accessed | tf_op | source)
XLA Modules:
  0.0 78.5 jit_solution(7106128905881958257)
XLA Ops:
  0.0 0.0 copy-start.6
  0.0 0.7 copy-done.6
  0.7 0.0 copy-start
  0.7 1.2 %copy-done = bf16[256,2048]{1,0:T(8,128)(2,1)S(1)} copy-done((bf16[256,2048]{1,0:T(8,128)(2,1)S(1)}, bf16[256,2048]{1,0:T(8,128)(2,1)}, u32[]{:S(2)}) %copy-start) | copy-done | bytes 1048600
  1.9 0.0 copy-start.1
  1.9 1.2 %copy-done.1 = bf16[512,1024]{1,0:T(8,128)(2,1)S(1)} copy-done((bf16[512,1024]{1,0:T(8,128)(2,1)S(1)}, bf16[512,1024]{1,0:T(8,128)(2,1)}, u32[]{:S(2)}) %copy-start.1) | copy-done | bytes 1048600
  3.1 0.0 copy-start.2
  3.1 1.2 %copy-done.2 = bf16[1024,512]{1,0:T(8,128)(2,1)S(1)} copy-done((bf16[1024,512]{1,0:T(8,128)(2,1)S(1)}, bf16[1024,512]{1,0:T(8,128)(2,1)}, u32[]{:S(2)}) %copy-start.2) | copy-done | bytes 1048600
  4.3 0.0 copy-start.3
  4.3 1.1 %copy-done.3 = bf16[1,512,3,256]{3,1,2,0:T(8,128)(2,1)S(1)} copy-done((bf16[1,512,3,256]{3,1,2,0:T(8,128)(2,1)S(1)}, bf16[1,512,3,256]{3,1,2,0:T(8,128)(2,1)}, u32[]{:S(2)}) %copy-start.3) | copy-done | bytes 786456
  5.5 0.0 copy-start.4
  5.5 0.9 %copy-done.4 = bf16[256,512]{1,0:T(8,128)(2,1)S(1)} copy-done((bf16[256,512]{1,0:T(8,128)(2,1)S(1)}, bf16[256,512]{1,0:T(8,128)(2,1)}, u32[]{:S(2)}) %copy-start.4) | copy-done | bytes 262168
  6.4 0.0 copy-start.5
  6.4 0.7 copy-done.5
  7.1 70.7 %shard_map.73 = bf16[64,2048]{1,0:T(8,128)(2,1)S(1)} custom-call(s32[1,24]{1,0:T(1,128)S(1)} %copy-done.6, f32[3,3,256]{2,1,0:T(4,128)S(1)} %copy-done.5, bf16[3,512,256]{2,1,0:T(8,128)(2,1)S(1)} %bitcast.5, bf16[256,512]{1,0:T(8,128)(2,1)S(1)} %copy-done.4, bf16[256,2048]{1,0:T(8,128)(2,1)S(1)} %copy-done, bf16[1024,512]{1,0:T(8,128)(2,1)S(1)} %copy-done.2, ...), custom_call_target="tpu_custom_call" | custom-call | tf_op jit(solution)/shard_map/pallas_call | solution.py:331
  77.8 0.7 copy.9
Async XLA Ops:
  0.0 0.7 copy-start.6
  0.7 1.2 %copy-start = (bf16[256,2048]{1,0:T(8,128)(2,1)S(1)}, bf16[256,2048]{1,0:T(8,128)(2,1)}, u32[]{:S(2)}) copy-start(bf16[256,2048]{1,0:T(8,128)(2,1)} %w.1) | copy-start | bytes 3145732
  1.9 1.2 %copy-start.1 = (bf16[512,1024]{1,0:T(8,128)(2,1)S(1)}, bf16[512,1024]{1,0:T(8,128)(2,1)}, u32[]{:S(2)}) copy-start(bf16[512,1024]{1,0:T(8,128)(2,1)} %constant.5.clone.inv) | copy-start | bytes 3145732
  3.1 1.2 %copy-start.2 = (bf16[1024,512]{1,0:T(8,128)(2,1)S(1)}, bf16[1024,512]{1,0:T(8,128)(2,1)}, u32[]{:S(2)}) copy-start(bf16[1024,512]{1,0:T(8,128)(2,1)} %constant.4.clone.fwd) | copy-start | bytes 3145732
  4.3 1.1 %copy-start.3 = (bf16[1,512,3,256]{3,1,2,0:T(8,128)(2,1)S(1)}, bf16[1,512,3,256]{3,1,2,0:T(8,128)(2,1)}, u32[]{:S(2)}) copy-start(bf16[1,512,3,256]{3,1,2,0:T(8,128)(2,1)} %param.7) | copy-start | bytes 2359300
  5.5 0.9 %copy-start.4 = (bf16[256,512]{1,0:T(8,128)(2,1)S(1)}, bf16[256,512]{1,0:T(8,128)(2,1)}, u32[]{:S(2)}) copy-start(bf16[256,512]{1,0:T(8,128)(2,1)} %filt.1) | copy-start | bytes 786436
  6.4 0.7 copy-start.5
where the time goes:
time: 78.9 us; the launch traced here: 78.5 us
  Pallas kernels  70.7 us (90%)
  local copies, waits for them, and re-layouts  7.82 us (10%)
    pallas_call x1, Pallas kernels, per_device(): pl.pallas_call(functools.partial(kernel, (n_ctx, n_ch, n_dp, block_len, d...  70.7 us
    unnamed x15, local copies, waits for them, and re-layouts  7.82 us

commit v1 on v0

--- a/solution.py
+++ b/solution.py
@@ -11,6 +11,7 @@
 MESH = pl.DeviceIdType.MESH
 F32 = jnp.float32
 BF16 = jnp.bfloat16
+SUBS = 8
 HALF = 128
 
 
@@ -24,8 +25,8 @@
 
 
 def kernel(
-    sizes, doc, taps, x, filt, w, fwd, inv, out,
-    ext, fbuf, ibuf, wbuf, pbuf, rbuf, tbuf, fspec, gspec, spec, qbuf, acc, total, cown, csend, crecv, gated, sbuf, vbuf,
+    sizes, doc_in, taps_in, x, filt, w, fwd, inv, out,
+    doc, taps, ext, fbuf, ibuf, wbuf, pbuf, rbuf, tbuf, fspec, gspec, spec, qbuf, acc, total, cown, csend, crecv, gated, sbuf, vbuf,
     load_sem, tail_sem, tap_send, tap_recv, halo_send, halo_recv, swap_send, swap_recv, ring_send, ring_recv,
 ):
     n_ctx, n_ch, n_dp, block_len, d_out = sizes
@@ -36,7 +37,8 @@
     z = ctx // 2
     c = ctx % 2
     piece = block_len // n_ch
-    sub = d_out // 4
+    sub = d_out // SUBS
+    order = [i // 2 + (i % 2) * (SUBS // 2) for i in range(SUBS)]
     steps = n_ch - 1
 
     def chip(distance):
@@ -44,9 +46,11 @@
 
     barrier = pltpu.get_barrier_semaphore()
     pl.semaphore_signal(barrier, inc=1, device_id={"context": 2 * z + 1 - c}, device_id_type=MESH)
-    for distance in (-1, -2):
-        for core in (0, 1):
-            pl.semaphore_signal(barrier, inc=1, device_id={"context": 2 * chip(distance) + core}, device_id_type=MESH)
+    for distance in (1, 2):
+        @pl.when(z >= distance)
+        def _():
+            for core in (0, 1):
+                pl.semaphore_signal(barrier, inc=1, device_id={"context": 2 * chip(-distance) + core}, device_id_type=MESH)
     for by in range(1, n_dp):
         pl.semaphore_signal(barrier, inc=1, device_id={"dp": lax.rem(xi + by, n_dp)}, device_id_type=MESH)
     for by in (1, n_ch - 1):
@@ -59,25 +63,19 @@
         pltpu.make_async_copy(fwd, fbuf, load_sem.at[2]),
         pltpu.make_async_copy(inv, ibuf, load_sem.at[3]),
         pltpu.make_async_copy(w, wbuf, load_sem.at[4]),
+        pltpu.make_async_copy(doc_in, doc, load_sem.at[5]),
+        pltpu.make_async_copy(taps_in, taps, load_sem.at[6]),
     ]
     for load in loads:
         load.start()
-    pl.semaphore_wait(barrier, 4 + n_dp + 2)
-
-    tail = pltpu.make_async_remote_copy(
-        src_ref=x.at[:, pl.ds(block_len - 16, 16), :], dst_ref=ext.at[:, pl.ds(0, 16), :],
-        send_sem=tail_sem.at[0], recv_sem=tail_sem.at[1],
-        device_id={"context": lax.rem(ctx + 1, n_ctx)}, device_id_type=MESH)
-    tail.start()
-
     def tap_copy(by):
         return pltpu.make_async_remote_copy(
             src_ref=filt.at[own_rows, :], dst_ref=tbuf.at[xi],
             send_sem=tap_send.at[by - 1], recv_sem=tap_recv.at[by - 1],
             device_id={"dp": lax.rem(xi + by, n_dp)}, device_id_type=MESH)
 
-    for by in range(1, n_dp):
-        tap_copy(by).start()
+    loads[5].wait()
+    loads[6].wait()
 
     def goes_on(block):
         at = jnp.maximum(block, 0)
@@ -92,8 +90,8 @@
 
     chunk = min(128, block_len)
 
-    def smooth(stream, start):
-        rows = ext[stream, pl.ds(start, chunk + 16), :].astype(F32)
+    def smooth(stream, start, count):
+        rows = ext[stream, pl.ds(start, count + 16), :].astype(F32)
         got = (
             taps[0, pl.ds(stream, 1), :] * rows
             + taps[1, pl.ds(stream, 1), :] * pltpu.roll(rows, 1, 0)
@@ -101,47 +99,89 @@
         )
         return got[16:]
 
-    def make_product(start):
-        product = (smooth(1, start) * smooth(2, start)).astype(BF16)
-        pbuf[0, pl.ds(start, chunk), :] = product[:, :HALF]
-        pbuf[1, pl.ds(start, chunk), :] = product[:, HALF:]
+    def make_product(start, count):
+        product = (smooth(1, start, count) * smooth(2, start, count)).astype(BF16)
+        pbuf[0, pl.ds(start, count), :] = product[:, :HALF]
+        pbuf[1, pl.ds(start, count), :] = product[:, HALF:]
+
+    def make_gate(start, count):
+        smoothed = smooth(0, start, count)
+        qbuf[0, pl.ds(start, count), :] = smoothed[:, :HALF]
+        qbuf[1, pl.ds(start, count), :] = smoothed[:, HALF:]
+
+    parts = (pl.ds(16, block_len - 16), pl.ds(0, 16))
+
+    def halo_copy(distance, half, part):
+        return pltpu.make_async_remote_copy(
+            src_ref=pbuf.at[half, parts[part], :], dst_ref=rbuf.at[distance, c, parts[part], :],
+            send_sem=halo_send.at[distance, half, part], recv_sem=halo_recv.at[distance, c, part],
+            device_id={"context": 2 * chip(distance) + half}, device_id_type=MESH)
+
+    def halo_arrived(distance, core):
+        for part in (0, 1):
+            pltpu.make_async_remote_copy(
+                src_ref=pbuf.at[0, parts[part], :], dst_ref=rbuf.at[distance, core, parts[part], :],
+                send_sem=halo_send.at[distance, 0, part], recv_sem=halo_recv.at[distance, core, part],
+                device_id={"context": ctx}, device_id_type=MESH).wait_recv()
+
+    def each_halo(act, parts_of):
+        for distance in (2, 1):
+            @pl.when(z + distance < chips)
+            def _():
+                for part in parts_of:
+                    for half in (0, 1):
+                        act(halo_copy(distance, half, part))
+        for part in parts_of:
+            act(halo_copy(0, 1 - c, part))
 
     loads[0].wait()
-    for start in range(chunk, block_len, chunk):
-        make_product(start)
-    tail.wait_recv()
+    for start in range(0, block_len, chunk):
+        first = max(start, 16)
+        make_product(first, start + chunk - first)
+
+    ahead = jnp.where(z + 1 < chips, 2, 0) + jnp.where(z + 2 < chips, 2, 0)
+    pl.semaphore_wait(barrier, 1 + ahead + (n_dp - 1) + 2)
+
+    tail = pltpu.make_async_remote_copy(
+        src_ref=x.at[:, pl.ds(block_len - 16, 16), :], dst_ref=ext.at[:, pl.ds(0, 16), :],
+        send_sem=tail_sem.at[0], recv_sem=tail_sem.at[1],
+        device_id={"context": lax.rem(ctx + 1, n_ctx)}, device_id_type=MESH)
+
+    @pl.when(ctx + 1 < n_ctx)
+    def _():
+        tail.start()
+
+    each_halo(lambda copy: copy.start(), (0,))
+    for by in range(1, n_dp):
+        tap_copy(by).start()
+
+    for start in range(0, block_len, chunk):
+        first = max(start, 16)
+        make_gate(first, start + chunk - first)
+    for distance in (1, 2):
+        @pl.when(z < distance)
+        def _():
+            rbuf[distance] = jnp.zeros(rbuf.shape[1:], BF16)
+
+    @pl.when(ctx > 0)
+    def _():
+        tail.wait_recv()
+
+    @pl.when(ctx == 0)
+    def _():
+        ext[:, pl.ds(0, 16), :] = jnp.zeros((3, 16, ext.shape[2]), BF16)
+
     for stream in range(3):
         ext[stream, pl.ds(0, 16), :] = (ext[stream, pl.ds(0, 16), :].astype(F32) * own_goes_on).astype(BF16)
-    make_product(0)
-
-    def halo_copy(distance, half):
-        return pltpu.make_async_remote_copy(
-            src_ref=pbuf.at[half], dst_ref=rbuf.at[distance, c],
-            send_sem=halo_send.at[distance, half], recv_sem=halo_recv.at[distance, c],
-            device_id={"context": 2 * chip(distance) + half}, device_id_type=MESH)
-
-    def halo_arrived(distance, core):
-        pltpu.make_async_remote_copy(
-            src_ref=pbuf.at[0], dst_ref=rbuf.at[distance, core],
-            send_sem=halo_send.at[distance, 0], recv_sem=halo_recv.at[distance, core],
-            device_id={"context": ctx}, device_id_type=MESH).wait_recv()
-
-    halo_copy(0, 1 - c).start()
-    for distance in (1, 2):
-        for half in (0, 1):
-            halo_copy(distance, half).start()
+    make_product(0, 16)
+    each_halo(lambda copy: copy.start(), (1,))
+    make_gate(0, 16)
     rbuf[0, c] = pbuf[c]
-
-    for start in range(0, block_len, chunk):
-        smoothed = smooth(0, start)
-        qbuf[0, pl.ds(start, chunk), :] = smoothed[:, :HALF]
-        qbuf[1, pl.ds(start, chunk), :] = smoothed[:, HALF:]
 
     loads[1].wait()
     loads[2].wait()
     for by in range(1, n_dp):
         tap_copy(by).wait_recv()
-    taps_all = tbuf[...].reshape(n_dp * HALF, block_len)
     tile = block_len // 2
 
     def filter_rows(i, carry):
@@ -206,8 +246,12 @@
 
     halo_arrived(0, 1 - c)
     transform(0, None, None)
-    for core in (0, 1):
-        halo_arrived(1, core)
+
+    @pl.when(z >= 1)
+    def _():
+        for core in (0, 1):
+            halo_arrived(1, core)
+
     transform(1, keep2, keep1)
 
     def early(i, carry):
@@ -221,8 +265,12 @@
         return carry
 
     lax.fori_loop(0, tiles, early, 0)
-    for core in (0, 1):
-        halo_arrived(2, core)
+
+    @pl.when(z >= 2)
+    def _():
+        for core in (0, 1):
+            halo_arrived(2, core)
+
     transform(2, keep4, keep3)
 
     def late(i, carry):
@@ -265,7 +313,7 @@
     loads[4].wait()
 
     def ring_copy(s, q):
-        to = lax.rem(y + (1 if q < 2 else n_ch - 1), n_ch)
+        to = lax.rem(y + (1 if q < SUBS // 2 else n_ch - 1), n_ch)
         return pltpu.make_async_remote_copy(
             src_ref=sbuf.at[s, q], dst_ref=vbuf.at[s, q],
             send_sem=ring_send.at[s, q], recv_sem=ring_recv.at[s, q],
@@ -279,8 +327,8 @@
     def ring_step(s, first):
         up = lax.rem(y - 1 - s + 2 * n_ch, n_ch)
         down = lax.rem(y + 1 + s, n_ch)
-        for q in (0, 2, 1, 3):
-            part = project(up if q < 2 else down, q)
+        for q in order:
+            part = project(up if q < SUBS // 2 else down, q)
             if not first:
                 ring_copy(s - 1, q).wait_recv()
                 part = part + vbuf[s - 1, q].astype(F32)
@@ -294,23 +342,23 @@
         return carry
 
     lax.fori_loop(1, steps, ring_body, 0)
-    for q in (0, 2, 1, 3):
+    for q in order:
         part = project(y, q)
         ring_copy(steps - 1, q).wait_recv()
         out[:, q * sub:(q + 1) * sub] = (part + vbuf[steps - 1, q].astype(F32)).astype(BF16)
 
-    tail.wait_send()
+    @pl.when(ctx + 1 < n_ctx)
+    def _():
+        tail.wait_send()
+
     for by in range(1, n_dp):
         tap_copy(by).wait_send()
-    halo_copy(0, 1 - c).wait_send()
-    for distance in (1, 2):
-        for half in (0, 1):
-            halo_copy(distance, half).wait_send()
+    each_halo(lambda copy: copy.wait_send(), (0, 1))
     for i in range(block_len // chunk):
         swap_copy(i).wait_send()
 
     def sent(s, carry):
-        for q in range(4):
+        for q in range(SUBS):
             ring_copy(s, q).wait_send()
         return carry
 
@@ -322,18 +370,20 @@
     n_ctx, n_ch, n_dp = mesh_shape["context"], mesh_shape["channel"], mesh_shape["dp"]
     streams = jnp.transpose(features[0], (1, 0, 2))
     forward, inverse = tables(block_len)
-    piece, sub, steps = block_len // n_ch, d_out // 4, n_ch - 1
+    piece, sub, steps = block_len // n_ch, d_out // SUBS, n_ch - 1
     width = 2 * block_len
     swaps = block_len // min(128, block_len)
-    anywhere = pl.BlockSpec(memory_space=pl.ANY)
+    anywhere = pl.BlockSpec(memory_space=pltpu.HBM)
     vmem = pl.BlockSpec(memory_space=pltpu.VMEM)
     dma = pltpu.SemaphoreType.DMA
     result = pl.pallas_call(
         functools.partial(kernel, (n_ctx, n_ch, n_dp, block_len, d_out)),
         out_shape=jax.ShapeDtypeStruct((piece, d_out), BF16),
-        in_specs=[pl.BlockSpec(memory_space=pltpu.SMEM), vmem] + [anywhere] * 5,
+        in_specs=[anywhere] * 7,
         out_specs=vmem,
         scratch_shapes=[
+            pltpu.SMEM(doc_start.shape, jnp.int32),
+            pltpu.VMEM(short_taps.shape, F32),
             pltpu.VMEM((3, 16 + block_len, channels), BF16),
             pltpu.VMEM((width, block_len), BF16),
             pltpu.VMEM((block_len, width), BF16),
@@ -351,13 +401,13 @@
             pltpu.VMEM((block_len, HALF), BF16),
             pltpu.VMEM((block_len, HALF), BF16),
             pltpu.VMEM((2, block_len, HALF), BF16),
-            pltpu.VMEM((steps, 4, piece, sub), BF16),
-            pltpu.VMEM((steps, 4, piece, sub), BF16),
-            dma((5,)), dma((2,)), dma((n_dp - 1,)), dma((n_dp - 1,)), dma((3, 2)), dma((3, 2)),
-            dma((swaps,)), dma((swaps,)), dma((steps, 4)), dma((steps, 4)),
+            pltpu.VMEM((steps, SUBS, piece, sub), BF16),
+            pltpu.VMEM((steps, SUBS, piece, sub), BF16),
+            dma((7,)), dma((2,)), dma((n_dp - 1,)), dma((n_dp - 1,)), dma((3, 2, 2)), dma((3, 2, 2)),
+            dma((swaps,)), dma((swaps,)), dma((steps, SUBS)), dma((steps, SUBS)),
         ],
         compiler_params=pltpu.CompilerParams(
-            collective_id=0, has_side_effects=True, vmem_limit_bytes=48 * 1024 * 1024),
+            collective_id=0, has_side_effects=True, vmem_limit_bytes=60 * 1024 * 1024),
     )(doc_start, short_taps, streams, long_filter, w_out, forward, inverse)
     return result[None]
 

time: 78.9 us -> 63.3 us (0.80)
  the two profiles are of different devices: /device:TPU:8 before, /device:TPU:256 now
where the time goes in v1:
time: 63.3 us; the launch traced here: 63.1 us
  Pallas kernels  61.5 us (97%)
  local copies, waits for them, and re-layouts  1.67 us (3%)
    pallas_call x1, Pallas kernels, per_device(): pl.pallas_call(functools.partial(kernel, (n_ctx, n_ch, n_dp, block_len, d...  61.5 us
    unnamed x1, local copies, waits for them, and re-layouts  1.67 us

profile of v1, /device:TPU:256, one launch (start us, length us, event | category | flops | bytes accessed | tf_op | source)
XLA Modules:
  0.0 63.1 jit_solution(6874009768461443565)
XLA Ops:
  0.0 61.5 %shard_map.73 = bf16[64,2048]{1,0:T(8,128)(2,1)} custom-call(s32[1,24]{1,0:T(1,128)} %doc_in.1, f32[3,3,256]{2,1,0:T(4,128)} %taps_in.1, bf16[3,512,256]{2,1,0:T(8,128)(2,1)} %bitcast.5, bf16[256,512]{1,0:T(8,128)(2,1)} %filt.1, bf16[256,2048]{1,0:T(8,128)(2,1)} %w.1, bf16[1024,512]{1,0:T(8,128)(2,1)} %constant.4.clone.fwd, bf16[512,1024]{1,0:T(8,128)(2,1)} %constant.5.clone.inv), custom_call_target="tpu_custom_call" | custom-call | tf_op jit(solution)/shard_map/pallas_call | solution.py:379
  61.5 1.7 %copy.9 = bf16[1,64,2048]{2,1,0:T(8,128)(2,1)} copy(bf16[1,64,2048]{2,1,0:T(8,128)(2,1)} %bitcast.4) | data formatting | bytes 524288

commit v2 on v1

--- a/solution.py
+++ b/solution.py
@@ -11,7 +11,6 @@
 MESH = pl.DeviceIdType.MESH
 F32 = jnp.float32
 BF16 = jnp.bfloat16
-SUBS = 8
 HALF = 128
 
 
@@ -26,8 +25,10 @@
 
 def kernel(
     sizes, doc_in, taps_in, x, filt, w, fwd, inv, out,
-    doc, taps, ext, fbuf, ibuf, wbuf, pbuf, rbuf, tbuf, fspec, gspec, spec, qbuf, acc, total, cown, csend, crecv, gated, sbuf, vbuf,
-    load_sem, tail_sem, tap_send, tap_recv, halo_send, halo_recv, swap_send, swap_recv, ring_send, ring_recv,
+    doc, taps, ext, fbuf, ibuf, wall, pbuf, rbuf, tbuf, fspec, gspec, spec, qbuf, qsend, acc, total,
+    gown, gall, gpair, osum, psend, precv, rsend, rrecv,
+    load_sem, tail_sem, tap_send, tap_recv, halo_send, halo_recv, q_sem, w_send, w_recv,
+    g_send, g_recv, f_send, f_recv, p_send, p_recv, r_sem,
 ):
     n_ctx, n_ch, n_dp, block_len, d_out = sizes
     chips = n_ctx // 2
@@ -37,15 +38,16 @@
     z = ctx // 2
     c = ctx % 2
     piece = block_len // n_ch
-    sub = d_out // SUBS
-    order = [i // 2 + (i % 2) * (SUBS // 2) for i in range(SUBS)]
-    steps = n_ch - 1
+    columns = d_out // 2
+    sibling = {"context": 2 * z + 1 - c}
+    side = xi % 2
+    partner = {"dp": xi + 1 - 2 * side}
 
     def chip(distance):
         return lax.rem(z + distance + chips, chips)
 
     barrier = pltpu.get_barrier_semaphore()
-    pl.semaphore_signal(barrier, inc=1, device_id={"context": 2 * z + 1 - c}, device_id_type=MESH)
+    pl.semaphore_signal(barrier, inc=1, device_id=sibling, device_id_type=MESH)
     for distance in (1, 2):
         @pl.when(z >= distance)
         def _():
@@ -53,7 +55,7 @@
                 pl.semaphore_signal(barrier, inc=1, device_id={"context": 2 * chip(-distance) + core}, device_id_type=MESH)
     for by in range(1, n_dp):
         pl.semaphore_signal(barrier, inc=1, device_id={"dp": lax.rem(xi + by, n_dp)}, device_id_type=MESH)
-    for by in (1, n_ch - 1):
+    for by in range(1, n_ch):
         pl.semaphore_signal(barrier, inc=1, device_id={"channel": lax.rem(y + by, n_ch)}, device_id_type=MESH)
 
     own_rows = pl.ds(pl.multiple_of(c * HALF, HALF), HALF)
@@ -62,7 +64,8 @@
         pltpu.make_async_copy(filt.at[own_rows, :], tbuf.at[xi], load_sem.at[1]),
         pltpu.make_async_copy(fwd, fbuf, load_sem.at[2]),
         pltpu.make_async_copy(inv, ibuf, load_sem.at[3]),
-        pltpu.make_async_copy(w, wbuf, load_sem.at[4]),
+        pltpu.make_async_copy(
+            w.at[own_rows, pl.ds(pl.multiple_of(side * columns, 128), columns)], wall.at[y], load_sem.at[4]),
         pltpu.make_async_copy(doc_in, doc, load_sem.at[5]),
         pltpu.make_async_copy(taps_in, taps, load_sem.at[6]),
     ]
@@ -105,9 +108,9 @@
         pbuf[1, pl.ds(start, count), :] = product[:, HALF:]
 
     def make_gate(start, count):
-        smoothed = smooth(0, start, count)
-        qbuf[0, pl.ds(start, count), :] = smoothed[:, :HALF]
-        qbuf[1, pl.ds(start, count), :] = smoothed[:, HALF:]
+        smoothed = smooth(0, start, count).astype(BF16)
+        qsend[0, pl.ds(start, count), :] = smoothed[:, :HALF]
+        qsend[1, pl.ds(start, count), :] = smoothed[:, HALF:]
 
     parts = (pl.ds(16, block_len - 16), pl.ds(0, 16))
 
@@ -140,7 +143,7 @@
         make_product(first, start + chunk - first)
 
     ahead = jnp.where(z + 1 < chips, 2, 0) + jnp.where(z + 2 < chips, 2, 0)
-    pl.semaphore_wait(barrier, 1 + ahead + (n_dp - 1) + 2)
+    pl.semaphore_wait(barrier, 1 + ahead + (n_dp - 1) + (n_ch - 1))
 
     tail = pltpu.make_async_remote_copy(
         src_ref=x.at[:, pl.ds(block_len - 16, 16), :], dst_ref=ext.at[:, pl.ds(0, 16), :],
@@ -152,6 +155,36 @@
         tail.start()
 
     each_halo(lambda copy: copy.start(), (0,))
+
+    w_steps = n_ch // 2
+
+    def w_copy(way, step):
+        by = (1, n_ch - 1)[way]
+        source = lax.rem(y + (n_ch - by) * (step - 1), n_ch)
+        lanes = pl.ds(0, columns) if step < w_steps else pl.ds(way * (columns // 2), columns // 2)
+        return pltpu.make_async_remote_copy(
+            src_ref=wall.at[source, :, lanes], dst_ref=wall.at[source, :, lanes],
+            send_sem=w_send.at[way, step - 1], recv_sem=w_recv.at[way, step - 1],
+            device_id={"channel": lax.rem(y + by, n_ch)}, device_id_type=MESH)
+
+    def w_arrived(way, step):
+        by = (1, n_ch - 1)[way]
+        source = lax.rem(y + (n_ch - by) * step, n_ch)
+        lanes = pl.ds(0, columns) if step < w_steps else pl.ds(way * (columns // 2), columns // 2)
+        pltpu.make_async_remote_copy(
+            src_ref=wall.at[source, :, lanes], dst_ref=wall.at[source, :, lanes],
+            send_sem=w_send.at[way, step - 1], recv_sem=w_recv.at[way, step - 1],
+            device_id={"channel": lax.rem(y + by, n_ch)}, device_id_type=MESH).wait_recv()
+
+    def pass_on(step):
+        if step < w_steps:
+            for way in (0, 1):
+                w_arrived(way, step)
+                w_copy(way, step + 1).start()
+
+    loads[4].wait()
+    for way in (0, 1):
+        w_copy(way, 1).start()
     for by in range(1, n_dp):
         tap_copy(by).start()
 
@@ -176,6 +209,11 @@
     make_product(0, 16)
     each_halo(lambda copy: copy.start(), (1,))
     make_gate(0, 16)
+    q_copy = pltpu.make_async_remote_copy(
+        src_ref=qsend.at[1 - c], dst_ref=qbuf.at[c], send_sem=q_sem.at[0], recv_sem=q_sem.at[1],
+        device_id=sibling, device_id_type=MESH)
+    q_copy.start()
+    qbuf[c] = qsend[c]
     rbuf[0, c] = pbuf[c]
 
     loads[1].wait()
@@ -217,6 +255,7 @@
         return carry
 
     lax.fori_loop(0, tiles, combine, 0)
+    pass_on(1)
 
     def transform(distance, keep_lo, keep_hi):
         lo, hi = rbuf[distance, 0], rbuf[distance, 1]
@@ -265,6 +304,7 @@
         return carry
 
     lax.fori_loop(0, tiles, early, 0)
+    pass_on(2)
 
     @pl.when(z >= 2)
     def _():
@@ -287,66 +327,101 @@
     lax.fori_loop(0, tiles, late, 0)
 
     loads[3].wait()
-
-    def swap_copy(i):
-        rows = pl.ds(i * chunk, chunk)
-        return pltpu.make_async_remote_copy(
-            src_ref=csend.at[rows, :], dst_ref=crecv.at[rows, :],
-            send_sem=swap_send.at[i], recv_sem=swap_recv.at[i],
-            device_id={"context": 2 * z + 1 - c}, device_id_type=MESH)
-
-    own_first = (1 - c).astype(F32)
-    own_second = c.astype(F32)
-    for i in range(block_len // chunk):
-        rows = pl.ds(i * chunk, chunk)
+    pltpu.make_async_remote_copy(
+        src_ref=qsend.at[1 - c], dst_ref=qbuf.at[1 - c], send_sem=q_sem.at[0], recv_sem=q_sem.at[1],
+        device_id=sibling, device_id_type=MESH).wait_recv()
+    pairs = n_ch // 2
+    own_pair = y // 2
+    other = y + 1 - 2 * (y % 2)
+
+    def g_copy(to):
+        return pltpu.make_async_remote_copy(
+            src_ref=gown.at[to], dst_ref=gall.at[y], send_sem=g_send.at[to], recv_sem=g_recv.at[y],
+            device_id={"channel": to}, device_id_type=MESH)
+
+    def g_arrived(source):
+        pltpu.make_async_remote_copy(
+            src_ref=gown.at[source], dst_ref=gall.at[source], send_sem=g_send.at[source], recv_sem=g_recv.at[source],
+            device_id={"channel": other}, device_id_type=MESH).wait_recv()
+
+    def f_copy(source):
+        return pltpu.make_async_remote_copy(
+            src_ref=gall.at[source], dst_ref=gpair.at[source], send_sem=f_send.at[source], recv_sem=f_recv.at[source],
+            device_id=partner, device_id_type=MESH)
+
+    for k in range(pairs):
+        pair = lax.rem(own_pair + k, pairs)
+        rows = pl.ds(pl.multiple_of(pair * 2 * piece, 2 * piece), 2 * piece)
         conv = jnp.dot(ibuf[rows, :], total[...], preferred_element_type=F32)
-        cown[0, rows, :] = conv[:, :HALF]
-        cown[1, rows, :] = conv[:, HALF:]
-        csend[rows, :] = cown[1 - c, rows, :].astype(BF16)
-        swap_copy(i).start()
-        gated[c, rows, :] = (qbuf[c, rows, :] * cown[c, rows, :]).astype(BF16)
-    for i in range(block_len // chunk):
-        rows = pl.ds(i * chunk, chunk)
-        swap_copy(i).wait_recv()
-        gated[1 - c, rows, :] = (qbuf[1 - c, rows, :] * crecv[rows, :].astype(F32)).astype(BF16)
-
-    loads[4].wait()
-
-    def ring_copy(s, q):
-        to = lax.rem(y + (1 if q < SUBS // 2 else n_ch - 1), n_ch)
-        return pltpu.make_async_remote_copy(
-            src_ref=sbuf.at[s, q], dst_ref=vbuf.at[s, q],
-            send_sem=ring_send.at[s, q], recv_sem=ring_recv.at[s, q],
-            device_id={"channel": to}, device_id_type=MESH)
-
-    def project(j, q):
-        rows = pl.ds(pl.multiple_of(j * piece, piece), piece)
-        lhs = jnp.concatenate([gated[0, rows, :], gated[1, rows, :]], 1)
-        return jnp.dot(lhs, wbuf[:, q * sub:(q + 1) * sub], preferred_element_type=F32)
-
-    def ring_step(s, first):
-        up = lax.rem(y - 1 - s + 2 * n_ch, n_ch)
-        down = lax.rem(y + 1 + s, n_ch)
-        for q in order:
-            part = project(up if q < SUBS // 2 else down, q)
-            if not first:
-                ring_copy(s - 1, q).wait_recv()
-                part = part + vbuf[s - 1, q].astype(F32)
-            sbuf[s, q] = part.astype(BF16)
-            ring_copy(s, q).start()
-
-    ring_step(0, True)
-
-    def ring_body(s, carry):
-        ring_step(s, False)
-        return carry
-
-    lax.fori_loop(1, steps, ring_body, 0)
-    for q in order:
-        part = project(y, q)
-        ring_copy(steps - 1, q).wait_recv()
-        out[:, q * sub:(q + 1) * sub] = (part + vbuf[steps - 1, q].astype(F32)).astype(BF16)
-
+        for block in (0, 1):
+            got = (qbuf[block, rows, :].astype(F32) * conv[:, block * HALF:(block + 1) * HALF]).astype(BF16)
+            for i in (0, 1):
+                gown[2 * pair + i, pl.ds(block * piece, piece), :] = got[i * piece:(i + 1) * piece]
+        if k == 0:
+            g_copy(other).start()
+            gall[y] = gown[y]
+            f_copy(y).start()
+        else:
+            for i in (0, 1):
+                g_copy(2 * pair + i).start()
+    pass_on(3)
+
+    for k in range(pairs):
+        pair = lax.rem(own_pair - k + pairs, pairs)
+        for source in (other,) if k == 0 else (2 * pair, 2 * pair + 1):
+            g_arrived(source)
+            f_copy(source).start()
+    for way in (0, 1):
+        w_arrived(way, w_steps)
+
+    mine = 2 * piece
+    for k in range(pairs):
+        pair = lax.rem(own_pair - k + pairs, pairs)
+        weights = jnp.concatenate([wall[2 * pair], wall[2 * pair + 1]], 0)
+        own = jnp.concatenate([gall[2 * pair], gall[2 * pair + 1]], 1)
+        for i in (0, 1):
+            f_copy(2 * pair + i).wait_recv()
+        theirs = jnp.concatenate([gpair[2 * pair], gpair[2 * pair + 1]], 1)
+        part = jnp.dot(jnp.concatenate([own, theirs], 0), weights, preferred_element_type=F32)
+        if k == 0:
+            osum[...] = part
+        else:
+            osum[...] += part
+
+    def p_copy(i):
+        return pltpu.make_async_remote_copy(
+            src_ref=psend.at[i], dst_ref=precv.at[i], send_sem=p_send.at[i], recv_sem=p_recv.at[i],
+            device_id=sibling, device_id_type=MESH)
+
+    def rows_of_block(whose, block):
+        return pl.ds(pl.multiple_of(whose * mine + block * piece, piece), piece)
+
+    for whose in (1, 0):
+        psend[whose] = osum[rows_of_block(whose, 1 - c), :].astype(BF16)
+        p_copy(whose).start()
+    back = pltpu.make_async_remote_copy(
+        src_ref=rsend, dst_ref=rrecv, send_sem=r_sem.at[0], recv_sem=r_sem.at[1],
+        device_id=partner, device_id_type=MESH)
+    p_copy(1).wait_recv()
+    rsend[...] = (osum[rows_of_block(1, c), :] + precv[1].astype(F32)).astype(BF16)
+    back.start()
+    p_copy(0).wait_recv()
+    out[:, pl.ds(pl.multiple_of(side * columns, 128), columns)] = (
+        osum[rows_of_block(0, c), :] + precv[0].astype(F32)).astype(BF16)
+    back.wait_recv()
+    out[:, pl.ds(pl.multiple_of((1 - side) * columns, 128), columns)] = rrecv[...]
+
+    back.wait_send()
+    q_copy.wait_send()
+    for whose in (1, 0):
+        p_copy(whose).wait_send()
+    for step in range(1, w_steps + 1):
+        for way in (0, 1):
+            w_copy(way, step).wait_send()
+    f_copy(y).wait_send()
+    for by in range(1, n_ch):
+        g_copy(lax.rem(y + by, n_ch)).wait_send()
+        f_copy(lax.rem(y + by, n_ch)).wait_send()
     @pl.when(ctx + 1 < n_ctx)
     def _():
         tail.wait_send()
@@ -354,15 +429,6 @@
     for by in range(1, n_dp):
         tap_copy(by).wait_send()
     each_halo(lambda copy: copy.wait_send(), (0, 1))
-    for i in range(block_len // chunk):
-        swap_copy(i).wait_send()
-
-    def sent(s, carry):
-        for q in range(SUBS):
-            ring_copy(s, q).wait_send()
-        return carry
-
-    lax.fori_loop(0, steps, sent, 0)
 
 
 def per_device(mesh_shape, features, doc_start, short_taps, long_filter, w_out):
@@ -370,9 +436,8 @@
     n_ctx, n_ch, n_dp = mesh_shape["context"], mesh_shape["channel"], mesh_shape["dp"]
     streams = jnp.transpose(features[0], (1, 0, 2))
     forward, inverse = tables(block_len)
-    piece, sub, steps = block_len // n_ch, d_out // SUBS, n_ch - 1
+    piece, columns = block_len // n_ch, d_out // 2
     width = 2 * block_len
-    swaps = block_len // min(128, block_len)
     anywhere = pl.BlockSpec(memory_space=pltpu.HBM)
     vmem = pl.BlockSpec(memory_space=pltpu.VMEM)
     dma = pltpu.SemaphoreType.DMA
@@ -387,24 +452,28 @@
             pltpu.VMEM((3, 16 + block_len, channels), BF16),
             pltpu.VMEM((width, block_len), BF16),
             pltpu.VMEM((block_len, width), BF16),
-            pltpu.VMEM((channels, d_out), BF16),
+            pltpu.VMEM((n_ch, HALF, columns), BF16),
             pltpu.VMEM((2, block_len, HALF), BF16),
             pltpu.VMEM((3, 2, block_len, HALF), BF16),
             pltpu.VMEM((n_dp, HALF, block_len), BF16),
             pltpu.VMEM((width, n_dp * HALF), F32),
             pltpu.VMEM((n_dp + 1, width, HALF), F32),
             pltpu.VMEM((3, width, 2 * HALF), F32),
-            pltpu.VMEM((2, block_len, HALF), F32),
+            pltpu.VMEM((2, block_len, HALF), BF16),
+            pltpu.VMEM((2, block_len, HALF), BF16),
             pltpu.VMEM((2, width, HALF), F32),
             pltpu.VMEM((width, 2 * HALF), BF16),
-            pltpu.VMEM((2, block_len, HALF), F32),
-            pltpu.VMEM((block_len, HALF), BF16),
-            pltpu.VMEM((block_len, HALF), BF16),
-            pltpu.VMEM((2, block_len, HALF), BF16),
-            pltpu.VMEM((steps, SUBS, piece, sub), BF16),
-            pltpu.VMEM((steps, SUBS, piece, sub), BF16),
-            dma((7,)), dma((2,)), dma((n_dp - 1,)), dma((n_dp - 1,)), dma((3, 2, 2)), dma((3, 2, 2)),
-            dma((swaps,)), dma((swaps,)), dma((steps, SUBS)), dma((steps, SUBS)),
+            pltpu.VMEM((n_ch, 2 * piece, HALF), BF16),
+            pltpu.VMEM((n_ch, 2 * piece, HALF), BF16),
+            pltpu.VMEM((n_ch, 2 * piece, HALF), BF16),
+            pltpu.VMEM((4 * piece, columns), F32),
+            pltpu.VMEM((2, piece, columns), BF16),
+            pltpu.VMEM((2, piece, columns), BF16),
+            pltpu.VMEM((piece, columns), BF16),
+            pltpu.VMEM((piece, columns), BF16),
+            dma((7,)), dma((2,)), dma((n_dp - 1,)), dma((n_dp - 1,)), dma((3, 2, 2)), dma((3, 2, 2)), dma((2,)),
+            dma((2, n_ch // 2)), dma((2, n_ch // 2)), dma((n_ch,)), dma((n_ch,)), dma((n_ch,)), dma((n_ch,)),
+            dma((2,)), dma((2,)), dma((2,)),
         ],
         compiler_params=pltpu.CompilerParams(
             collective_id=0, has_side_effects=True, vmem_limit_bytes=60 * 1024 * 1024),

time: 63.3 us -> 57.3 us (0.905)
  the two profiles are of different devices: /device:TPU:256 before, /device:TPU:195 now
where the time goes in v2:
time: 57.3 us; the launch traced here: 57.2 us
  Pallas kernels  55.5 us (97%)
  local copies, waits for them, and re-layouts  1.67 us (3%)
    pallas_call x1, Pallas kernels, per_device(): pl.pallas_call(functools.partial(kernel, (n_ctx, n_ch, n_dp, block_len, d...  55.5 us
    unnamed x1, local copies, waits for them, and re-layouts  1.67 us

profile of v2, /device:TPU:195, one launch (start us, length us, event | category | flops | bytes accessed | tf_op | source)
XLA Modules:
  0.0 57.2 jit_solution(17779222047896007702)
XLA Ops:
  0.0 55.5 %shard_map.73 = bf16[64,2048]{1,0:T(8,128)(2,1)} custom-call(s32[1,24]{1,0:T(1,128)} %doc_in.1, f32[3,3,256]{2,1,0:T(4,128)} %taps_in.1, bf16[3,512,256]{2,1,0:T(8,128)(2,1)} %bitcast.5, bf16[256,512]{1,0:T(8,128)(2,1)} %filt.1, bf16[256,2048]{1,0:T(8,128)(2,1)} %w.1, bf16[1024,512]{1,0:T(8,128)(2,1)} %constant.4.clone.fwd, bf16[512,1024]{1,0:T(8,128)(2,1)} %constant.5.clone.inv), custom_call_target="tpu_custom_call" | custom-call | tf_op jit(solution)/shard_map/pallas_call | solution.py:444
  55.5 1.7 %copy.9 = bf16[1,64,2048]{2,1,0:T(8,128)(2,1)} copy(bf16[1,64,2048]{2,1,0:T(8,128)(2,1)} %bitcast.4) | data formatting | bytes 524288

commit v3 on v2

--- a/solution.py
+++ b/solution.py
@@ -25,10 +25,10 @@
 
 def kernel(
     sizes, doc_in, taps_in, x, filt, w, fwd, inv, out,
-    doc, taps, ext, fbuf, ibuf, wall, pbuf, rbuf, tbuf, fspec, gspec, spec, qbuf, qsend, acc, total,
+    doc, taps, ext, fbuf, ibuf, wall, pbuf, rbuf, tbuf, both, fspec, gspec, spec, qbuf, qsend, acc, total,
     gown, gall, gpair, osum, psend, precv, rsend, rrecv,
-    load_sem, tail_sem, tap_send, tap_recv, halo_send, halo_recv, q_sem, w_send, w_recv,
-    g_send, g_recv, f_send, f_recv, p_send, p_recv, r_sem,
+    load_sem, tail_sem, tap_send, tap_recv, halo_send, halo_recv, q_sem, w_send, w_recv, m_send, m_recv,
+    g_send, g_recv, f_send, f_recv, p_send, p_recv, r_send, r_recv,
 ):
     n_ctx, n_ch, n_dp, block_len, d_out = sizes
     chips = n_ctx // 2
@@ -40,19 +40,22 @@
     piece = block_len // n_ch
     columns = d_out // 2
     sibling = {"context": 2 * z + 1 - c}
-    side = xi % 2
-    partner = {"dp": xi + 1 - 2 * side}
+    odd = xi % 2
+    side = ((xi + 1) // 2) % 2
+    partner = {"dp": xi + 1 - 2 * odd}
+    mate = {"dp": lax.rem(xi + 2 * odd - 1 + n_dp, n_dp)}
 
     def chip(distance):
         return lax.rem(z + distance + chips, chips)
 
     barrier = pltpu.get_barrier_semaphore()
     pl.semaphore_signal(barrier, inc=1, device_id=sibling, device_id_type=MESH)
-    for distance in (1, 2):
-        @pl.when(z >= distance)
-        def _():
-            for core in (0, 1):
-                pl.semaphore_signal(barrier, inc=1, device_id={"context": 2 * chip(-distance) + core}, device_id_type=MESH)
+
+    @pl.when(z >= 1)
+    def _():
+        for core in (0, 1):
+            pl.semaphore_signal(barrier, inc=1, device_id={"context": 2 * chip(-1) + core}, device_id_type=MESH)
+
     for by in range(1, n_dp):
         pl.semaphore_signal(barrier, inc=1, device_id={"dp": lax.rem(xi + by, n_dp)}, device_id_type=MESH)
     for by in range(1, n_ch):
@@ -112,7 +115,8 @@
         qsend[0, pl.ds(start, count), :] = smoothed[:, :HALF]
         qsend[1, pl.ds(start, count), :] = smoothed[:, HALF:]
 
-    parts = (pl.ds(16, block_len - 16), pl.ds(0, 16))
+    middle = block_len // 2
+    parts = (pl.ds(16, middle - 16), pl.ds(middle, middle), pl.ds(0, 16))
 
     def halo_copy(distance, half, part):
         return pltpu.make_async_remote_copy(
@@ -120,29 +124,49 @@
             send_sem=halo_send.at[distance, half, part], recv_sem=halo_recv.at[distance, c, part],
             device_id={"context": 2 * chip(distance) + half}, device_id_type=MESH)
 
-    def halo_arrived(distance, core):
-        for part in (0, 1):
-            pltpu.make_async_remote_copy(
-                src_ref=pbuf.at[0, parts[part], :], dst_ref=rbuf.at[distance, core, parts[part], :],
-                send_sem=halo_send.at[distance, 0, part], recv_sem=halo_recv.at[distance, core, part],
-                device_id={"context": ctx}, device_id_type=MESH).wait_recv()
+    def forward_copy(core, part):
+        return pltpu.make_async_remote_copy(
+            src_ref=rbuf.at[1, core, parts[part], :], dst_ref=rbuf.at[2, core, parts[part], :],
+            send_sem=halo_send.at[2, core, part], recv_sem=halo_recv.at[2, core, part],
+            device_id={"context": 2 * chip(1) + c}, device_id_type=MESH)
+
+    def halo_arrived(distance, core, part):
+        pltpu.make_async_remote_copy(
+            src_ref=pbuf.at[0, parts[part], :], dst_ref=rbuf.at[distance, core, parts[part], :],
+            send_sem=halo_send.at[distance, 0, part], recv_sem=halo_recv.at[distance, core, part],
+            device_id=sibling, device_id_type=MESH).wait_recv()
 
     def each_halo(act, parts_of):
-        for distance in (2, 1):
-            @pl.when(z + distance < chips)
-            def _():
-                for part in parts_of:
-                    for half in (0, 1):
-                        act(halo_copy(distance, half, part))
+        @pl.when(z + 1 < chips)
+        def _():
+            for part in parts_of:
+                for half in (0, 1):
+                    act(halo_copy(1, half, part))
+
         for part in parts_of:
             act(halo_copy(0, 1 - c, part))
 
+    def take_in(parts_of):
+        @pl.when(z >= 1)
+        def _():
+            for part in parts_of:
+                for core in (0, 1):
+                    halo_arrived(1, core, part)
+
+        @pl.when((z >= 1) & (z + 1 < chips))
+        def _():
+            for part in parts_of:
+                for core in (0, 1):
+                    forward_copy(core, part).start()
+
+    def make_products(lo, hi):
+        for start in range(lo, hi, chunk):
+            first = max(start, 16)
+            make_product(first, start + chunk - first)
+
     loads[0].wait()
-    for start in range(0, block_len, chunk):
-        first = max(start, 16)
-        make_product(first, start + chunk - first)
-
-    ahead = jnp.where(z + 1 < chips, 2, 0) + jnp.where(z + 2 < chips, 2, 0)
+    make_products(0, 0 * chunk)
+    ahead = jnp.where(z + 1 < chips, 2, 0)
     pl.semaphore_wait(barrier, 1 + ahead + (n_dp - 1) + (n_ch - 1))
 
     tail = pltpu.make_async_remote_copy(
@@ -154,39 +178,46 @@
     def _():
         tail.start()
 
-    each_halo(lambda copy: copy.start(), (0,))
 
     w_steps = n_ch // 2
 
-    def w_copy(way, step):
+    quarter = columns // 4
+
+    def w_link(way, step, arriving):
         by = (1, n_ch - 1)[way]
-        source = lax.rem(y + (n_ch - by) * (step - 1), n_ch)
-        lanes = pl.ds(0, columns) if step < w_steps else pl.ds(way * (columns // 2), columns // 2)
-        return pltpu.make_async_remote_copy(
+        source = lax.rem(y + (n_ch - by) * (step if arriving else step - 1), n_ch)
+        start, count = odd * quarter, 3 * quarter
+        if step == w_steps:
+            count = count // 2
+            start = start + way * count
+        lanes = pl.ds(pl.multiple_of(start, 128), count)
+        return source, pltpu.make_async_remote_copy(
             src_ref=wall.at[source, :, lanes], dst_ref=wall.at[source, :, lanes],
             send_sem=w_send.at[way, step - 1], recv_sem=w_recv.at[way, step - 1],
             device_id={"channel": lax.rem(y + by, n_ch)}, device_id_type=MESH)
 
-    def w_arrived(way, step):
-        by = (1, n_ch - 1)[way]
-        source = lax.rem(y + (n_ch - by) * step, n_ch)
-        lanes = pl.ds(0, columns) if step < w_steps else pl.ds(way * (columns // 2), columns // 2)
-        pltpu.make_async_remote_copy(
+    def m_copy(source, arriving):
+        lanes = pl.ds(pl.multiple_of(((1 - odd) if arriving else odd) * 3 * quarter, 128), quarter)
+        return pltpu.make_async_remote_copy(
             src_ref=wall.at[source, :, lanes], dst_ref=wall.at[source, :, lanes],
-            send_sem=w_send.at[way, step - 1], recv_sem=w_recv.at[way, step - 1],
-            device_id={"channel": lax.rem(y + by, n_ch)}, device_id_type=MESH).wait_recv()
+            send_sem=m_send.at[source], recv_sem=m_recv.at[source], device_id=mate, device_id_type=MESH)
 
     def pass_on(step):
         if step < w_steps:
             for way in (0, 1):
-                w_arrived(way, step)
-                w_copy(way, step + 1).start()
+                source, arrival = w_link(way, step, True)
+                arrival.wait_recv()
+                w_link(way, step + 1, False)[1].start()
+                m_copy(source, False).start()
 
     loads[4].wait()
     for way in (0, 1):
-        w_copy(way, 1).start()
+        w_link(way, 1, False)[1].start()
     for by in range(1, n_dp):
         tap_copy(by).start()
+
+    make_products(0 * chunk, block_len)
+    each_halo(lambda copy: copy.start(), (0, 1))
 
     for start in range(0, block_len, chunk):
         first = max(start, 16)
@@ -207,7 +238,7 @@
     for stream in range(3):
         ext[stream, pl.ds(0, 16), :] = (ext[stream, pl.ds(0, 16), :].astype(F32) * own_goes_on).astype(BF16)
     make_product(0, 16)
-    each_halo(lambda copy: copy.start(), (1,))
+    each_halo(lambda copy: copy.start(), (2,))
     make_gate(0, 16)
     q_copy = pltpu.make_async_remote_copy(
         src_ref=qsend.at[1 - c], dst_ref=qbuf.at[c], send_sem=q_sem.at[0], recv_sem=q_sem.at[1],
@@ -216,6 +247,8 @@
     qbuf[c] = qsend[c]
     rbuf[0, c] = pbuf[c]
 
+    pass_on(1)
+
     loads[1].wait()
     loads[2].wait()
     for by in range(1, n_dp):
@@ -228,7 +261,9 @@
             fbuf[rows, :], tbuf[...].reshape(n_dp * HALF, block_len), (((1,), (1,)), ((), ())), preferred_element_type=F32)
         return carry
 
+    take_in((0,))
     lax.fori_loop(0, 4, filter_rows, 0)
+    take_in((1, 2))
 
     step_rows = min(64, block_len // 2)
     tiles = block_len // step_rows
@@ -255,20 +290,18 @@
         return carry
 
     lax.fori_loop(0, tiles, combine, 0)
-    pass_on(1)
 
     def transform(distance, keep_lo, keep_hi):
         lo, hi = rbuf[distance, 0], rbuf[distance, 1]
         if keep_lo is not None:
             lo = (lo.astype(F32) * keep_lo).astype(BF16)
             hi = (hi.astype(F32) * keep_hi).astype(BF16)
-        rbuf[distance, 0] = lo
-        rbuf[distance, 1] = hi
+        both[:, :HALF] = lo
+        both[:, HALF:] = hi
 
         def rows_of(i, carry):
             rows = pl.ds(pl.multiple_of(i * tile, tile), tile)
-            both = jnp.concatenate([rbuf[distance, 0], rbuf[distance, 1]], 1)
-            spec[distance, rows, :] = jnp.dot(fbuf[rows, :], both, preferred_element_type=F32)
+            spec[distance, rows, :] = jnp.dot(fbuf[rows, :], both[...], preferred_element_type=F32)
             return carry
 
         lax.fori_loop(0, 4, rows_of, 0)
@@ -283,14 +316,9 @@
         got = [term(d, distance, core, re, im) for d, distance, core in which]
         return sum(g[0] for g in got[1:]) + got[0][0], sum(g[1] for g in got[1:]) + got[0][1]
 
-    halo_arrived(0, 1 - c)
+    for part in (0, 1, 2):
+        halo_arrived(0, 1 - c, part)
     transform(0, None, None)
-
-    @pl.when(z >= 1)
-    def _():
-        for core in (0, 1):
-            halo_arrived(1, core)
-
     transform(1, keep2, keep1)
 
     def early(i, carry):
@@ -308,8 +336,9 @@
 
     @pl.when(z >= 2)
     def _():
-        for core in (0, 1):
-            halo_arrived(2, core)
+        for part in (0, 1, 2):
+            for core in (0, 1):
+                halo_arrived(2, core, part)
 
     transform(2, keep4, keep3)
 
@@ -366,61 +395,100 @@
                 g_copy(2 * pair + i).start()
     pass_on(3)
 
-    for k in range(pairs):
+    def pieces(k):
         pair = lax.rem(own_pair - k + pairs, pairs)
-        for source in (other,) if k == 0 else (2 * pair, 2 * pair + 1):
+        return 2 * pair, 2 * pair + 1
+
+    def hand_on(k):
+        for source in (other,) if k == 0 else pieces(k):
             g_arrived(source)
             f_copy(source).start()
-    for way in (0, 1):
-        w_arrived(way, w_steps)
-
-    mine = 2 * piece
-    for k in range(pairs):
-        pair = lax.rem(own_pair - k + pairs, pairs)
-        weights = jnp.concatenate([wall[2 * pair], wall[2 * pair + 1]], 0)
-        own = jnp.concatenate([gall[2 * pair], gall[2 * pair + 1]], 1)
-        for i in (0, 1):
-            f_copy(2 * pair + i).wait_recv()
-        theirs = jnp.concatenate([gpair[2 * pair], gpair[2 * pair + 1]], 1)
-        part = jnp.dot(jnp.concatenate([own, theirs], 0), weights, preferred_element_type=F32)
+
+    def tokens(k):
+        first, second = pieces(k)
+        own = jnp.concatenate([gall[first], gall[second]], 1)
+        for source in (first, second):
+            f_copy(source).wait_recv()
+        return jnp.concatenate([own, jnp.concatenate([gpair[first], gpair[second]], 1)], 0)
+
+    def weights(k, lanes):
+        first, second = pieces(k)
+        return jnp.concatenate([wall[first, :, lanes], wall[second, :, lanes]], 0)
+
+    def project(k):
+        part = jnp.dot(tokens(k), weights(k, slice(None)), preferred_element_type=F32)
         if k == 0:
             osum[...] = part
         else:
             osum[...] += part
 
-    def p_copy(i):
-        return pltpu.make_async_remote_copy(
-            src_ref=psend.at[i], dst_ref=precv.at[i], send_sem=p_send.at[i], recv_sem=p_recv.at[i],
+    hand_on(0)
+    hand_on(1)
+    for way in (0, 1):
+        w_link(way, w_steps, True)[1].wait_recv()
+    m_copy(lax.rem(y + w_steps, n_ch), False).start()
+    for by in range(1, n_ch):
+        m_copy(lax.rem(y + by, n_ch), True).wait_recv()
+    for k in range(pairs - 1):
+        project(k)
+        if k + 2 < pairs:
+            hand_on(k + 2)
+
+    mine = 2 * piece
+    part_columns = columns // 2
+
+    def p_copy(whose, h):
+        return pltpu.make_async_remote_copy(
+            src_ref=psend.at[whose, h], dst_ref=precv.at[whose, h],
+            send_sem=p_send.at[whose, h], recv_sem=p_recv.at[whose, h],
             device_id=sibling, device_id_type=MESH)
+
+    def back_copy(h):
+        return pltpu.make_async_remote_copy(
+            src_ref=rsend.at[h], dst_ref=rrecv.at[h], send_sem=r_send.at[h], recv_sem=r_recv.at[h],
+            device_id=partner, device_id_type=MESH)
 
     def rows_of_block(whose, block):
         return pl.ds(pl.multiple_of(whose * mine + block * piece, piece), piece)
 
-    for whose in (1, 0):
-        psend[whose] = osum[rows_of_block(whose, 1 - c), :].astype(BF16)
-        p_copy(whose).start()
-    back = pltpu.make_async_remote_copy(
-        src_ref=rsend, dst_ref=rrecv, send_sem=r_sem.at[0], recv_sem=r_sem.at[1],
-        device_id=partner, device_id_type=MESH)
-    p_copy(1).wait_recv()
-    rsend[...] = (osum[rows_of_block(1, c), :] + precv[1].astype(F32)).astype(BF16)
-    back.start()
-    p_copy(0).wait_recv()
-    out[:, pl.ds(pl.multiple_of(side * columns, 128), columns)] = (
-        osum[rows_of_block(0, c), :] + precv[0].astype(F32)).astype(BF16)
-    back.wait_recv()
-    out[:, pl.ds(pl.multiple_of((1 - side) * columns, 128), columns)] = rrecv[...]
-
-    back.wait_send()
+    last = tokens(pairs - 1)
+    for h in (0, 1):
+        lanes = pl.ds(h * part_columns, part_columns)
+        osum[:, lanes] += jnp.dot(last, weights(pairs - 1, lanes), preferred_element_type=F32)
+        for whose in (1, 0):
+            psend[whose, h] = osum[rows_of_block(whose, 1 - c), lanes].astype(BF16)
+            p_copy(whose, h).start()
+
+    def whole(whose, h):
+        p_copy(whose, h).wait_recv()
+        lanes = pl.ds(h * part_columns, part_columns)
+        return (osum[rows_of_block(whose, c), lanes] + precv[whose, h].astype(F32)).astype(BF16)
+
+    def out_lanes(which, h):
+        return pl.ds(pl.multiple_of(which * columns + h * part_columns, 128), part_columns)
+
+    for h in (0, 1):
+        rsend[h] = whole(1, h)
+        back_copy(h).start()
+    for h in (0, 1):
+        out[:, out_lanes(side, h)] = whole(0, h)
+    for h in (0, 1):
+        back_copy(h).wait_recv()
+        out[:, out_lanes(1 - side, h)] = rrecv[h]
+
+    for h in (0, 1):
+        back_copy(h).wait_send()
     q_copy.wait_send()
     for whose in (1, 0):
-        p_copy(whose).wait_send()
+        for h in (0, 1):
+            p_copy(whose, h).wait_send()
     for step in range(1, w_steps + 1):
         for way in (0, 1):
-            w_copy(way, step).wait_send()
+            w_link(way, step, False)[1].wait_send()
     f_copy(y).wait_send()
     for by in range(1, n_ch):
         g_copy(lax.rem(y + by, n_ch)).wait_send()
+        m_copy(lax.rem(y + by, n_ch), False).wait_send()
         f_copy(lax.rem(y + by, n_ch)).wait_send()
     @pl.when(ctx + 1 < n_ctx)
     def _():
@@ -428,7 +496,13 @@
 
     for by in range(1, n_dp):
         tap_copy(by).wait_send()
-    each_halo(lambda copy: copy.wait_send(), (0, 1))
+    each_halo(lambda copy: copy.wait_send(), (0, 1, 2))
+
+    @pl.when((z >= 1) & (z + 1 < chips))
+    def _():
+        for part in (0, 1, 2):
+            for core in (0, 1):
+                forward_copy(core, part).wait_send()
 
 
 def per_device(mesh_shape, features, doc_start, short_taps, long_filter, w_out):
@@ -456,6 +530,7 @@
             pltpu.VMEM((2, block_len, HALF), BF16),
             pltpu.VMEM((3, 2, block_len, HALF), BF16),
             pltpu.VMEM((n_dp, HALF, block_len), BF16),
+            pltpu.VMEM((block_len, 2 * HALF), BF16),
             pltpu.VMEM((width, n_dp * HALF), F32),
             pltpu.VMEM((n_dp + 1, width, HALF), F32),
             pltpu.VMEM((3, width, 2 * HALF), F32),
@@ -467,13 +542,13 @@
             pltpu.VMEM((n_ch, 2 * piece, HALF), BF16),
             pltpu.VMEM((n_ch, 2 * piece, HALF), BF16),
             pltpu.VMEM((4 * piece, columns), F32),
-            pltpu.VMEM((2, piece, columns), BF16),
-            pltpu.VMEM((2, piece, columns), BF16),
-            pltpu.VMEM((piece, columns), BF16),
-            pltpu.VMEM((piece, columns), BF16),
-            dma((7,)), dma((2,)), dma((n_dp - 1,)), dma((n_dp - 1,)), dma((3, 2, 2)), dma((3, 2, 2)), dma((2,)),
-            dma((2, n_ch // 2)), dma((2, n_ch // 2)), dma((n_ch,)), dma((n_ch,)), dma((n_ch,)), dma((n_ch,)),
-            dma((2,)), dma((2,)), dma((2,)),
+            pltpu.VMEM((2, 2, piece, columns // 2), BF16),
+            pltpu.VMEM((2, 2, piece, columns // 2), BF16),
+            pltpu.VMEM((2, piece, columns // 2), BF16),
+            pltpu.VMEM((2, piece, columns // 2), BF16),
+            dma((7,)), dma((2,)), dma((n_dp - 1,)), dma((n_dp - 1,)), dma((3, 2, 3)), dma((3, 2, 3)), dma((2,)),
+            dma((2, n_ch // 2)), dma((2, n_ch // 2)), dma((n_ch,)), dma((n_ch,)), dma((n_ch,)), dma((n_ch,)), dma((n_ch,)), dma((n_ch,)),
+            dma((2, 2)), dma((2, 2)), dma((2,)), dma((2,)),
         ],
         compiler_params=pltpu.CompilerParams(
             collective_id=0, has_side_effects=True, vmem_limit_bytes=60 * 1024 * 1024),

time: 57.3 us -> 52.7 us (0.920)
  the two profiles are of different devices: /device:TPU:195 before, /device:TPU:1 now
where the time goes in v3:
time: 52.7 us; the launch traced here: 52.3 us
  Pallas kernels  50.7 us (96%)
  local copies, waits for them, and re-layouts  1.67 us (3%)
    pallas_call x1, Pallas kernels, per_device(): pl.pallas_call(functools.partial(kernel, (n_ctx, n_ch, n_dp, block_len, d...  50.7 us
    unnamed x1, local copies, waits for them, and re-layouts  1.67 us

profile of v3, /device:TPU:1, one launch (start us, length us, event | category | flops | bytes accessed | tf_op | source)
XLA Modules:
  0.0 52.3 jit_solution(11206569105390150611)
XLA Ops:
  0.0 50.7 %shard_map.73 = bf16[64,2048]{1,0:T(8,128)(2,1)} custom-call(s32[1,24]{1,0:T(1,128)} %doc_in.1, f32[3,3,256]{2,1,0:T(4,128)} %taps_in.1, bf16[3,512,256]{2,1,0:T(8,128)(2,1)} %bitcast.5, bf16[256,512]{1,0:T(8,128)(2,1)} %filt.1, bf16[256,2048]{1,0:T(8,128)(2,1)} %w.1, bf16[1024,512]{1,0:T(8,128)(2,1)} %constant.4.clone.fwd, bf16[512,1024]{1,0:T(8,128)(2,1)} %constant.5.clone.inv), custom_call_target="tpu_custom_call" | custom-call | tf_op jit(solution)/shard_map/pallas_call | solution.py:518
  50.7 1.7 %copy.9 = bf16[1,64,2048]{2,1,0:T(8,128)(2,1)} copy(bf16[1,64,2048]{2,1,0:T(8,128)(2,1)} %bitcast.4) | data formatting | bytes 524288

commit v4 on v3

--- a/solution.py
+++ b/solution.py
@@ -27,7 +27,7 @@
     sizes, doc_in, taps_in, x, filt, w, fwd, inv, out,
     doc, taps, ext, fbuf, ibuf, wall, pbuf, rbuf, tbuf, both, fspec, gspec, spec, qbuf, qsend, acc, total,
     gown, gall, gpair, osum, psend, precv, rsend, rrecv,
-    load_sem, tail_sem, tap_send, tap_recv, halo_send, halo_recv, q_sem, w_send, w_recv, m_send, m_recv,
+    load_sem, tail_sem, tap_send, tap_recv, halo_send, halo_recv, q_sem, w_send, w_recv, e_send, e_recv, m_send, m_recv, u_send, u_recv,
     g_send, g_recv, f_send, f_recv, p_send, p_recv, r_send, r_recv,
 ):
     n_ctx, n_ch, n_dp, block_len, d_out = sizes
@@ -56,6 +56,10 @@
         for core in (0, 1):
             pl.semaphore_signal(barrier, inc=1, device_id={"context": 2 * chip(-1) + core}, device_id_type=MESH)
 
+    @pl.when(z + 1 < chips)
+    def _():
+        pl.semaphore_signal(barrier, inc=1, device_id={"context": 2 * chip(1) + c}, device_id_type=MESH)
+
     for by in range(1, n_dp):
         pl.semaphore_signal(barrier, inc=1, device_id={"dp": lax.rem(xi + by, n_dp)}, device_id_type=MESH)
     for by in range(1, n_ch):
@@ -166,7 +170,7 @@
 
     loads[0].wait()
     make_products(0, 0 * chunk)
-    ahead = jnp.where(z + 1 < chips, 2, 0)
+    ahead = jnp.where(z + 1 < chips, 2, 0) + jnp.where(z >= 1, 1, 0)
     pl.semaphore_wait(barrier, 1 + ahead + (n_dp - 1) + (n_ch - 1))
 
     tail = pltpu.make_async_remote_copy(
@@ -183,24 +187,49 @@
 
     quarter = columns // 4
 
-    def w_link(way, step, arriving):
+    level = z % 2
+    half_of = (odd + level) % 2
+    given = 2 * half_of + level
+    from_mate = 2 * (1 - half_of) + level
+    from_next = 2 * (1 - half_of) + 1 - level
+
+    def ring_link(way, step, arriving, start, count, send, recv):
         by = (1, n_ch - 1)[way]
         source = lax.rem(y + (n_ch - by) * (step if arriving else step - 1), n_ch)
-        start, count = odd * quarter, 3 * quarter
         if step == w_steps:
             count = count // 2
             start = start + way * count
         lanes = pl.ds(pl.multiple_of(start, 128), count)
         return source, pltpu.make_async_remote_copy(
             src_ref=wall.at[source, :, lanes], dst_ref=wall.at[source, :, lanes],
-            send_sem=w_send.at[way, step - 1], recv_sem=w_recv.at[way, step - 1],
+            send_sem=send.at[way, step - 1], recv_sem=recv.at[way, step - 1],
             device_id={"channel": lax.rem(y + by, n_ch)}, device_id_type=MESH)
 
+    def w_link(way, step, arriving):
+        return ring_link(way, step, arriving, half_of * 2 * quarter, 2 * quarter, w_send, w_recv)
+
+    def e_link(way, step, arriving):
+        return ring_link(way, step, arriving, from_next * quarter, quarter, e_send, e_recv)
+
+    def quarter_copy(source, place, send, recv, to):
+        lanes = pl.ds(pl.multiple_of(place * quarter, 128), quarter)
+        return pltpu.make_async_remote_copy(
+            src_ref=wall.at[source, :, lanes], dst_ref=wall.at[source, :, lanes],
+            send_sem=send.at[source], recv_sem=recv.at[source], device_id=to, device_id_type=MESH)
+
     def m_copy(source, arriving):
-        lanes = pl.ds(pl.multiple_of(((1 - odd) if arriving else odd) * 3 * quarter, 128), quarter)
-        return pltpu.make_async_remote_copy(
-            src_ref=wall.at[source, :, lanes], dst_ref=wall.at[source, :, lanes],
-            send_sem=m_send.at[source], recv_sem=m_recv.at[source], device_id=mate, device_id_type=MESH)
+        return quarter_copy(source, from_mate if arriving else given, m_send, m_recv, mate)
+
+    def u_copy(source, arriving):
+        return quarter_copy(
+            source, from_next if arriving else given, u_send, u_recv, {"context": 2 * chip(-1) + c})
+
+    def give(source):
+        m_copy(source, False).start()
+
+        @pl.when(z >= 1)
+        def _():
+            u_copy(source, False).start()
 
     def pass_on(step):
         if step < w_steps:
@@ -208,11 +237,23 @@
                 source, arrival = w_link(way, step, True)
                 arrival.wait_recv()
                 w_link(way, step + 1, False)[1].start()
-                m_copy(source, False).start()
+                give(source)
+
+            @pl.when(z + 1 == chips)
+            def _():
+                for way in (0, 1):
+                    e_link(way, step, True)[1].wait_recv()
+                    e_link(way, step + 1, False)[1].start()
 
     loads[4].wait()
     for way in (0, 1):
         w_link(way, 1, False)[1].start()
+
+    @pl.when(z + 1 == chips)
+    def _():
+        for way in (0, 1):
+            e_link(way, 1, False)[1].start()
+
     for by in range(1, n_dp):
         tap_copy(by).start()
 
@@ -264,6 +305,7 @@
     take_in((0,))
     lax.fori_loop(0, 4, filter_rows, 0)
     take_in((1, 2))
+    pass_on(2)
 
     step_rows = min(64, block_len // 2)
     tiles = block_len // step_rows
@@ -332,7 +374,7 @@
         return carry
 
     lax.fori_loop(0, tiles, early, 0)
-    pass_on(2)
+    pass_on(3)
 
     @pl.when(z >= 2)
     def _():
@@ -393,7 +435,10 @@
         else:
             for i in (0, 1):
                 g_copy(2 * pair + i).start()
-    pass_on(3)
+
+    for way in (0, 1):
+        w_link(way, w_steps, True)[1].wait_recv()
+    give(lax.rem(y + w_steps, n_ch))
 
     def pieces(k):
         pair = lax.rem(own_pair - k + pairs, pairs)
@@ -424,15 +469,24 @@
 
     hand_on(0)
     hand_on(1)
-    for way in (0, 1):
-        w_link(way, w_steps, True)[1].wait_recv()
-    m_copy(lax.rem(y + w_steps, n_ch), False).start()
+    hand_on(2)
     for by in range(1, n_ch):
         m_copy(lax.rem(y + by, n_ch), True).wait_recv()
+
+    @pl.when(z + 1 < chips)
+    def _():
+        for by in range(1, n_ch):
+            u_copy(lax.rem(y + by, n_ch), True).wait_recv()
+
+    @pl.when(z + 1 == chips)
+    def _():
+        for way in (0, 1):
+            e_link(way, w_steps, True)[1].wait_recv()
+
     for k in range(pairs - 1):
         project(k)
-        if k + 2 < pairs:
-            hand_on(k + 2)
+        if k + 3 < pairs:
+            hand_on(k + 3)
 
     mine = 2 * piece
     part_columns = columns // 2
@@ -486,6 +540,18 @@
         for way in (0, 1):
             w_link(way, step, False)[1].wait_send()
     f_copy(y).wait_send()
+
+    @pl.when(z >= 1)
+    def _():
+        for by in range(1, n_ch):
+            u_copy(lax.rem(y + by, n_ch), False).wait_send()
+
+    @pl.when(z + 1 == chips)
+    def _():
+        for step in range(1, w_steps + 1):
+            for way in (0, 1):
+                e_link(way, step, False)[1].wait_send()
+
     for by in range(1, n_ch):
         g_copy(lax.rem(y + by, n_ch)).wait_send()
         m_copy(lax.rem(y + by, n_ch), False).wait_send()
@@ -547,7 +613,8 @@
             pltpu.VMEM((2, piece, columns // 2), BF16),
             pltpu.VMEM((2, piece, columns // 2), BF16),
             dma((7,)), dma((2,)), dma((n_dp - 1,)), dma((n_dp - 1,)), dma((3, 2, 3)), dma((3, 2, 3)), dma((2,)),
-            dma((2, n_ch // 2)), dma((2, n_ch // 2)), dma((n_ch,)), dma((n_ch,)), dma((n_ch,)), dma((n_ch,)), dma((n_ch,)), dma((n_ch,)),
+            dma((2, n_ch // 2)), dma((2, n_ch // 2)), dma((2, n_ch // 2)), dma((2, n_ch // 2)),
+            dma((n_ch,)), dma((n_ch,)), dma((n_ch,)), dma((n_ch,)), dma((n_ch,)), dma((n_ch,)), dma((n_ch,)), dma((n_ch,)),
             dma((2, 2)), dma((2, 2)), dma((2,)), dma((2,)),
         ],
         compiler_params=pltpu.CompilerParams(

time: 52.7 us -> 49.8 us (0.945)
  Pallas kernels: 50.7 us -> 47.9 us
    pallas_call x1, Pallas kernels: 50.7 us -> 47.9 us  [per_device(): pl.pallas_call(functools.partial(kernel, (n_ctx, n_ch, n_dp, block_len, d...]
where the time goes in v4:
time: 49.8 us; the launch traced here: 49.6 us
  Pallas kernels  47.9 us (96%)
  local copies, waits for them, and re-layouts  1.67 us (3%)
    pallas_call x1, Pallas kernels, per_device(): pl.pallas_call(functools.partial(kernel, (n_ctx, n_ch, n_dp, block_len, d...  47.9 us
    unnamed x1, local copies, waits for them, and re-layouts  1.67 us

profile of v4, /device:TPU:1, one launch (start us, length us, event | category | flops | bytes accessed | tf_op | source)
XLA Modules:
  0.0 49.6 jit_solution(13404891274921564393)
XLA Ops:
  0.0 47.9 %shard_map.73 = bf16[64,2048]{1,0:T(8,128)(2,1)} custom-call(s32[1,24]{1,0:T(1,128)} %doc_in.1, f32[3,3,256]{2,1,0:T(4,128)} %taps_in.1, bf16[3,512,256]{2,1,0:T(8,128)(2,1)} %bitcast.5, bf16[256,512]{1,0:T(8,128)(2,1)} %filt.1, bf16[256,2048]{1,0:T(8,128)(2,1)} %w.1, bf16[1024,512]{1,0:T(8,128)(2,1)} %constant.4.clone.fwd, bf16[512,1024]{1,0:T(8,128)(2,1)} %constant.5.clone.inv), custom_call_target="tpu_custom_call" | custom-call | tf_op jit(solution)/shard_map/pallas_call | solution.py:584
  47.9 1.7 %copy.9 = bf16[1,64,2048]{2,1,0:T(8,128)(2,1)} copy(bf16[1,64,2048]{2,1,0:T(8,128)(2,1)} %bitcast.4) | data formatting | bytes 524288

commit v5 on v4

--- a/solution.py
+++ b/solution.py
@@ -169,7 +169,10 @@
             make_product(first, start + chunk - first)
 
     loads[0].wait()
-    make_products(0, 0 * chunk)
+    make_products(0, block_len)
+    for start in range(0, block_len, chunk):
+        first = max(start, 16)
+        make_gate(first, start + chunk - first)
     ahead = jnp.where(z + 1 < chips, 2, 0) + jnp.where(z >= 1, 1, 0)
     pl.semaphore_wait(barrier, 1 + ahead + (n_dp - 1) + (n_ch - 1))
 
@@ -234,10 +237,8 @@
     def pass_on(step):
         if step < w_steps:
             for way in (0, 1):
-                source, arrival = w_link(way, step, True)
-                arrival.wait_recv()
+                w_link(way, step, True)[1].wait_recv()
                 w_link(way, step + 1, False)[1].start()
-                give(source)
 
             @pl.when(z + 1 == chips)
             def _():
@@ -245,6 +246,9 @@
                     e_link(way, step, True)[1].wait_recv()
                     e_link(way, step + 1, False)[1].start()
 
+            for way in (0, 1):
+                give(lax.rem(y + (n_ch - (1, n_ch - 1)[way]) * step, n_ch))
+
     loads[4].wait()
     for way in (0, 1):
         w_link(way, 1, False)[1].start()
@@ -257,12 +261,8 @@
     for by in range(1, n_dp):
         tap_copy(by).start()
 
-    make_products(0 * chunk, block_len)
     each_halo(lambda copy: copy.start(), (0, 1))
 
-    for start in range(0, block_len, chunk):
-        first = max(start, 16)
-        make_gate(first, start + chunk - first)
     for distance in (1, 2):
         @pl.when(z < distance)
         def _():
@@ -304,8 +304,8 @@
 
     take_in((0,))
     lax.fori_loop(0, 4, filter_rows, 0)
+    pass_on(2)
     take_in((1, 2))
-    pass_on(2)
 
     step_rows = min(64, block_len // 2)
     tiles = block_len // step_rows

time: 49.8 us -> 49.7 us (level)
  no operation moved by 1% of the time
where the time goes in v5:
time: 49.7 us; the launch traced here: 49.5 us
  Pallas kernels  47.8 us (96%)
  local copies, waits for them, and re-layouts  1.67 us (3%)
    pallas_call x1, Pallas kernels, per_device(): pl.pallas_call(functools.partial(kernel, (n_ctx, n_ch, n_dp, block_len, d...  47.8 us
    unnamed x1, local copies, waits for them, and re-layouts  1.67 us

profile of v5, /device:TPU:1, one launch (start us, length us, event | category | flops | bytes accessed | tf_op | source)
XLA Modules:
  0.0 49.5 jit_solution(15479460669894440669)
XLA Ops:
  0.0 47.8 %shard_map.73 = bf16[64,2048]{1,0:T(8,128)(2,1)} custom-call(s32[1,24]{1,0:T(1,128)} %doc_in.1, f32[3,3,256]{2,1,0:T(4,128)} %taps_in.1, bf16[3,512,256]{2,1,0:T(8,128)(2,1)} %bitcast.5, bf16[256,512]{1,0:T(8,128)(2,1)} %filt.1, bf16[256,2048]{1,0:T(8,128)(2,1)} %w.1, bf16[1024,512]{1,0:T(8,128)(2,1)} %constant.4.clone.fwd, bf16[512,1024]{1,0:T(8,128)(2,1)} %constant.5.clone.inv), custom_call_target="tpu_custom_call" | custom-call | tf_op jit(solution)/shard_map/pallas_call | solution.py:584
  47.8 1.7 %copy.9 = bf16[1,64,2048]{2,1,0:T(8,128)(2,1)} copy(bf16[1,64,2048]{2,1,0:T(8,128)(2,1)} %bitcast.4) | data formatting | bytes 524288

commit v6 on v5

--- a/solution.py
+++ b/solution.py
@@ -470,20 +470,22 @@
     hand_on(0)
     hand_on(1)
     hand_on(2)
-    for by in range(1, n_ch):
-        m_copy(lax.rem(y + by, n_ch), True).wait_recv()
-
-    @pl.when(z + 1 < chips)
-    def _():
-        for by in range(1, n_ch):
-            u_copy(lax.rem(y + by, n_ch), True).wait_recv()
-
-    @pl.when(z + 1 == chips)
-    def _():
-        for way in (0, 1):
-            e_link(way, w_steps, True)[1].wait_recv()
+    def weights_here(k):
+        for source in (other,) if k == 0 else pieces(k):
+            m_copy(source, True).wait_recv()
+
+            @pl.when(z + 1 < chips)
+            def _():
+                u_copy(source, True).wait_recv()
+
+        if k == pairs // 2:
+            @pl.when(z + 1 == chips)
+            def _():
+                for way in (0, 1):
+                    e_link(way, w_steps, True)[1].wait_recv()
 
     for k in range(pairs - 1):
+        weights_here(k)
         project(k)
         if k + 3 < pairs:
             hand_on(k + 3)
@@ -505,6 +507,7 @@
     def rows_of_block(whose, block):
         return pl.ds(pl.multiple_of(whose * mine + block * piece, piece), piece)
 
+    weights_here(pairs - 1)
     last = tokens(pairs - 1)
     for h in (0, 1):
         lanes = pl.ds(h * part_columns, part_columns)

time: 49.7 us -> 49.7 us (level)
  no operation moved by 1% of the time
where the time goes in v6:
time: 49.7 us; the launch traced here: 49.5 us
  Pallas kernels  47.8 us (96%)
  local copies, waits for them, and re-layouts  1.67 us (3%)
    pallas_call x1, Pallas kernels, per_device(): pl.pallas_call(functools.partial(kernel, (n_ctx, n_ch, n_dp, block_len, d...  47.8 us
    unnamed x1, local copies, waits for them, and re-layouts  1.67 us

profile of v6, /device:TPU:1, one launch (start us, length us, event | category | flops | bytes accessed | tf_op | source)
XLA Modules:
  0.0 49.5 jit_solution(16181192308641118434)
XLA Ops:
  0.0 47.8 %shard_map.73 = bf16[64,2048]{1,0:T(8,128)(2,1)} custom-call(s32[1,24]{1,0:T(1,128)} %doc_in.1, f32[3,3,256]{2,1,0:T(4,128)} %taps_in.1, bf16[3,512,256]{2,1,0:T(8,128)(2,1)} %bitcast.5, bf16[256,512]{1,0:T(8,128)(2,1)} %filt.1, bf16[256,2048]{1,0:T(8,128)(2,1)} %w.1, bf16[1024,512]{1,0:T(8,128)(2,1)} %constant.4.clone.fwd, bf16[512,1024]{1,0:T(8,128)(2,1)} %constant.5.clone.inv), custom_call_target="tpu_custom_call" | custom-call | tf_op jit(solution)/shard_map/pallas_call | solution.py:587
  47.8 1.7 %copy.9 = bf16[1,64,2048]{2,1,0:T(8,128)(2,1)} copy(bf16[1,64,2048]{2,1,0:T(8,128)(2,1)} %bitcast.4) | data formatting | bytes 524288
